TPU v7x, 128 devices: a whole 4x4x4 slice. The times are simulated.
128 devices in a mesh: lon: 16 (over y, z_lo, core), lat: 8 (over x, z_hi).
Axes of the slice: x: 4, y: 4, z: 4 (z_hi: 2, z_lo: 2; z = z_hi * 2 + z_lo), core: 2. Of those that a mesh axis runs over, the one named last changes fastest.
Arguments:
- ocean_state: float32 [4, 4, 1024, 16384], P(None, None, 'lat', 'lon'), may hold values from -3 to 3
- depth_levels: int32 [1024, 16384], P('lat', 'lon'), may hold values from 0 to 4
- vert_mix: float32 [4, 1024, 16384], P(None, 'lat', 'lon'), may hold values from 0.1 to 4
- partner: int32 [16384], P('lon'), may hold values from 0 to 16383, as said below
- ice_velocity: float32 [2, 1024, 16384], P(None, 'lat', 'lon'), may hold values from -4 to 4
- ice_mass: float32 [1024, 16384], P('lat', 'lon'), may hold values from 0.2 to 2
- ice_strength: float32 [1024, 16384], P('lat', 'lon'), may hold values from 0.2 to 2
- ice_mask: int32 [1024, 16384], P('lat', 'lon'), may hold values 0 or 1
- ice_owned: int32 [8, 16, 3], P('lat', 'lon'), may hold values from -1 to 127, as said below
Outputs:
- new_tracers: float32 [2, 4, 1024, 16384], P(None, None, 'lat', 'lon')
- new_ice_velocity: float32 [2, 1024, 16384], P(None, 'lat', 'lon')
Inputs may be any that keep to these rules, and one draw needn't show every extreme that they name: partner[i] = (s - i) mod 16384 for one s drawn afresh; the partner of a column's partner is the column itself. `ice_owned`: entry [r, d, k] is -1 or a tile column of tile row r that lies on lon index (d - k) mod 16, that is, one of the 8 tile columns from ((d - k) mod 16) * 8 on; each tile column appears at most once in a row; in every row some lon index has all 3 slots filled and some lon index has none.
All inputs are finite; a program needn't handle non-finite values. No bound on the sum of `ice_mask` on one device may be relied on, other than what follows from the above.
Results may differ from a plain program's by a relative error of at most 0.0003.
Values sent between devices are 32-bit elements; how exact they have to be, the bound alone decides.
A program may use at most 192 MiB of HBM per device.

v0:
```python
import jax
import jax.numpy as jnp
from jax import lax
from jax.experimental import pallas as pl
from jax.experimental.pallas import tpu as pltpu
from jax.sharding import PartitionSpec as P

MESH = pl.DeviceIdType.MESH
LEV = 4
TILE = 128
ROWS = 128
COLS = 1024
LT = COLS // TILE
SLOTS = 3
SUBCYCLES = 32
NB = ROWS // 8
F32 = jnp.float32
I32 = jnp.int32


def iotas():
    lane = lax.broadcasted_iota(I32, (8, 128), 1)
    row = lax.broadcasted_iota(I32, (8, 128), 0)
    return lane, row


def ice_tile(pos, slot, ue_v, un_v, mass_v, str_v, mask_v, depth_v, uo_v, vo_v, stage, con, st, res_ref):
    lane, row = iotas()
    for b in range(NB):
        rows = slice(b * 8, b * 8 + 8)
        mass, strength = mass_v[pos, rows, :], str_v[pos, rows, :]
        ice = jnp.logical_and(mask_v[pos, rows, :] > 0, depth_v[pos, rows, :] > 0)
        stage[0, rows, :] = ue_v[pos, rows, :]
        stage[1, rows, :] = un_v[pos, rows, :]
        stage[2, rows, :] = jnp.where(ice, mass, 0.0)
        stage[3, rows, :] = jnp.where(ice, strength, 0.0)
        stage[4, rows, :] = uo_v[pos, rows, :]
        stage[5, rows, :] = vo_v[pos, rows, :]

    def strided(f, k):
        return stage[f, pl.ds(k, 8, stride=NB), :]

    p_south = None
    for k in range(NB):
        m = strided(2, k)
        strength = strided(3, k)
        inertia = m * 2.0
        a = inertia + 1.0
        b = m * 0.5
        inv = 1.0 / (a * a + b * b)
        p4 = strength * 0.25
        if k == 0:
            p_south = jnp.where(row == 0, 0.0, pltpu.roll(strided(3, NB - 1) * 0.25, 1, 0))
        p_west = jnp.where(lane == 0, 0.0, pltpu.roll(p4, 1, 1))
        con[0, k] = inertia
        con[1, k] = a * inv
        con[2, k] = b * inv
        con[3, k] = strength * (1.0 / 12.0)
        con[4, k] = strided(4, k) * 0.5 - (p4 - p_west)
        con[5, k] = strided(5, k) * 0.5 - (p4 - p_south)
        st[0, k] = strided(0, k) * 0.5
        st[1, k] = strided(1, k) * 0.5
        st[2, k] = p4
        st[3, k] = p4
        st[4, k] = jnp.zeros((8, 128), F32)
        p_south = p4

    keep = 1.0 / 1.5

    def momentum(k, u, v, sx, sy, sh, sy_s, sh_s):
        sx_w = jnp.where(lane == 0, 0.0, pltpu.roll(sx, 1, 1))
        sh_w = jnp.where(lane == 0, 0.0, pltpu.roll(sh, 1, 1))
        rx = (con[0, k] * u + con[4, k]) + ((sx - sx_w) + (sh - sh_s))
        ry = (con[0, k] * v + con[5, k]) + ((sh - sh_w) + (sy - sy_s))
        al, be = con[1, k], con[2, k]
        st[0, k] = al * rx + be * ry
        st[1, k] = al * ry - be * rx

    def cycle(_, carry):
        un, vn = st[0, 0], st[1, 0]
        u0, v0 = un, vn
        first = None
        sy_s = sh_s = None
        for k in range(NB):
            u, v = un, vn
            if k < NB - 1:
                un, vn = st[0, k + 1], st[1, k + 1]
            else:
                un = jnp.where(row == 7, 0.0, pltpu.roll(u0, 7, 0))
                vn = jnp.where(row == 7, 0.0, pltpu.roll(v0, 7, 0))
            ue = jnp.where(lane == 127, 0.0, pltpu.roll(u, 127, 1))
            ve = jnp.where(lane == 127, 0.0, pltpu.roll(v, 127, 1))
            d1 = ue - u
            d2 = vn - v
            h = (un - u) + (ve - v)
            div = d1 + d2
            ten = d1 - d2
            p = div + div
            r = ten * 0.5
            x = (p * p + ten * ten) + (h * h + 0.25)
            q = con[3, k] * lax.rsqrt(x)
            sx = st[2, k] * keep + q * (p + r)
            sy = st[3, k] * keep + q * (p - r)
            sh = st[4, k] * keep + q * h
            st[2, k] = sx
            st[3, k] = sy
            st[4, k] = sh
            if k == 0:
                first = (u, v, sx, sy, sh)
            else:
                momentum(k, u, v, sx, sy, sh, sy_s, sh_s)
            sy_s, sh_s = sy, sh
        sy_s = jnp.where(row == 0, 0.0, pltpu.roll(sy_s, 1, 0))
        sh_s = jnp.where(row == 0, 0.0, pltpu.roll(sh_s, 1, 0))
        momentum(0, *first, sy_s, sh_s)
        return carry

    lax.fori_loop(0, SUBCYCLES, cycle, 0)
    for k in range(NB):
        res_ref[slot, 0, pl.ds(k, 8, stride=NB), :] = st[0, k] * 2.0
        res_ref[slot, 1, pl.ds(k, 8, stride=NB), :] = st[1, k] * 2.0


def exchange_kernel(
    n_lon,
    n_lat,
    owned,
    state,
    depth,
    ivel,
    mass,
    strength,
    mask,
    he,
    hw,
    hs,
    hn,
    fold,
    res,
    info,
    depth_v,
    uo_v,
    vo_v,
    ue_v,
    un_v,
    mass_v,
    str_v,
    mask_v,
    col_first,
    col_last,
    blk_first,
    blk_last,
    pack_first,
    pack_last,
    pack_n,
    pack_s,
    pack_f,
    my_list,
    lists,
    lists_s,
    stage,
    con,
    st,
    load_sem,
    send_sem,
    recv_sem,
    fsend_sem,
    frecv_sem,
    local_sem,
    plane_sem,
):
    x = lax.axis_index("lon")
    y = lax.axis_index("lat")
    lane, row = iotas()
    top = y == n_lat - 1
    bottom = y == 0

    def lon(step):
        return {"lon": lax.rem(x + step + n_lon, n_lon), "lat": y}

    def lat(step):
        return {"lon": x, "lat": y + step}

    barrier = pltpu.get_barrier_semaphore()

    def greet(device):
        pl.semaphore_signal(barrier, inc=1, device_id=device, device_id_type=MESH)

    for step in (1, -1, 2, -2):
        greet(lon(step))

    @pl.when(top)
    def _():
        for step in range(3, n_lon - 2):
            greet(lon(step))

    @pl.when(jnp.logical_not(top))
    def _():
        greet(lat(1))

    @pl.when(jnp.logical_not(bottom))
    def _():
        greet(lat(-1))

    loads = [
        (state.at[0:2, :, :, pl.ds(0, 128)], col_first),
        (state.at[0:3, :, :, pl.ds(COLS - 128, 128)], col_last),
        (state.at[0:2, :, pl.ds(0, 8), :], blk_first),
        (state.at[0:2, :, pl.ds(ROWS - 8, 8), :], blk_last.at[0:2]),
        (state.at[3, :, pl.ds(ROWS - 8, 8), :], blk_last.at[2]),
    ]
    planes = [
        (depth, depth_v),
        (ivel.at[0], ue_v),
        (ivel.at[1], un_v),
        (mass, mass_v),
        (strength, str_v),
        (mask, mask_v),
        (state.at[2, 0], uo_v),
        (state.at[3, 0], vo_v),
    ]
    copies = [pltpu.make_async_copy(s, d, load_sem.at[i]) for i, (s, d) in enumerate(loads)]
    for i, (s, d) in enumerate(planes):
        if i == 1:
            for c in copies:
                c.start()
        for j in range(LT):
            pltpu.make_async_copy(s.at[:, j * 128 : j * 128 + 128], d.at[j], plane_sem.at[i]).start()

    def plane_wait(i):
        pltpu.make_async_copy(planes[i][1], planes[i][1], plane_sem.at[i]).wait()

    my_list[...] = jnp.where(
        lane == 0, owned[0, 0, 0], jnp.where(lane == 1, owned[0, 0, 1], owned[0, 0, 2])
    )

    plane_wait(0)
    for c in copies:
        c.wait()

    def pack_cols(b, carry):
        rows = pl.ds(pl.multiple_of(b * 8, 8), 8)
        first = jnp.zeros((8, 128), F32)
        last = jnp.zeros((8, 128), F32)
        for t in range(2):
            for k in range(LEV):
                n = t * LEV + k
                value = col_first[t, k, rows, :]
                first = jnp.where(lane == n, value if n == 0 else pltpu.roll(value, n, 1), first)
                last = jnp.where(lane == n, pltpu.roll(col_last[t, k, rows, :], n + 1, 1), last)
        d_first = depth_v[0, rows, :].astype(F32)
        d_last = depth_v[LT - 1, rows, :].astype(F32)
        first = jnp.where(lane == 8, pltpu.roll(d_first, 8, 1), first)
        last = jnp.where(lane == 8, pltpu.roll(d_last, 9, 1), last)
        for k in range(LEV):
            last = jnp.where(lane == 9 + k, pltpu.roll(col_last[2, k, rows, :], 10 + k, 1), last)
        pack_first[rows, :] = first
        pack_last[rows, :] = last
        return carry

    lax.fori_loop(0, NB, pack_cols, 0)
    pack_n[...] = jnp.zeros((16, COLS), F32)
    pack_s[...] = jnp.zeros((16, COLS), F32)
    for t in range(2):
        for k in range(LEV):
            n = t * LEV + k
            pack_n[n : n + 1, :] = blk_first[t, k, 0:1, :]
            pack_s[n : n + 1, :] = blk_last[t, k, 7:8, :]
    for k in range(LEV):
        pack_s[9 + k : 10 + k, :] = blk_last[2, k, 7:8, :]
    for j in range(LT):
        cols = slice(j * 128, j * 128 + 128)
        pack_n[8:9, cols] = depth_v[j, 0:8, :].astype(F32)[0:1, :]
        pack_s[8:9, cols] = depth_v[j, ROWS - 8 : ROWS, :].astype(F32)[7:8, :]
        pack_f[j] = pack_s[0:8, j * 128 : j * 128 + 128]
        pack_f[LT, j : j + 1, :] = pack_s[8:9, j * 128 : j * 128 + 128]

    @pl.when(jnp.logical_and(top, jnp.logical_not(bottom)))
    def _():
        pl.semaphore_wait(barrier, n_lon)

    @pl.when(jnp.logical_and(bottom, jnp.logical_not(top)))
    def _():
        pl.semaphore_wait(barrier, 5)

    @pl.when(jnp.logical_not(jnp.logical_or(bottom, top)))
    def _():
        pl.semaphore_wait(barrier, 6)

    def remote(src, dst, i, device):
        return pltpu.make_async_remote_copy(
            src_ref=src,
            dst_ref=dst,
            send_sem=send_sem.at[i],
            recv_sem=recv_sem.at[i],
            device_id=device,
            device_id_type=MESH,
        )

    list_1 = remote(my_list, lists.at[0], 0, lon(-1))
    list_2 = remote(my_list, lists.at[1], 1, lon(-2))
    to_west = remote(pack_first, he, 2, lon(-1))
    to_east = remote(pack_last, hw, 3, lon(1))
    to_south = remote(pack_n, hn, 4, lat(-1))
    to_north = remote(pack_s, hs, 5, lat(1))
    always = (list_1, list_2, to_west, to_east)
    for c in always:
        c.start()

    @pl.when(jnp.logical_not(bottom))
    def _():
        to_south.start()

    @pl.when(jnp.logical_not(top))
    def _():
        to_north.start()

    def fold_copy(step):
        return pltpu.make_async_remote_copy(
            src_ref=pack_f,
            dst_ref=fold.at[x],
            send_sem=fsend_sem.at[step],
            recv_sem=frecv_sem.at[x],
            device_id=lon(step),
            device_id_type=MESH,
        )

    def fold_arrival(step):
        source = lax.rem(x - step + n_lon, n_lon)
        return pltpu.make_async_remote_copy(
            src_ref=pack_f,
            dst_ref=fold.at[source],
            send_sem=fsend_sem.at[step],
            recv_sem=frecv_sem.at[source],
            device_id=lon(step),
            device_id_type=MESH,
        )

    own_fold = pltpu.make_async_copy(pack_f, fold.at[x], local_sem.at[0])

    @pl.when(top)
    def _():
        own_fold.start()
        for step in range(1, n_lon):
            fold_copy(step).start()

    for i in range(1, len(planes)):
        plane_wait(i)

    def work(column, slot):
        info[slot] = jnp.where(column >= 0, column - x * LT, -1)
        pos = jnp.clip(column - x * LT, 0, LT - 1)
        ice_tile(pos, slot, ue_v, un_v, mass_v, str_v, mask_v, depth_v, uo_v, vo_v, stage, con, st, res)

    work(owned[0, 0, 0], 0)
    list_1.wait_recv()
    list_2.wait_recv()
    to_smem = pltpu.make_async_copy(lists, lists_s, local_sem.at[1])
    to_smem.start()
    to_smem.wait()
    work(lists_s[0, 0, 1], 1)
    work(lists_s[1, 0, 2], 2)

    list_1.wait_send()
    list_2.wait_send()
    to_west.wait()
    to_east.wait()

    @pl.when(jnp.logical_not(bottom))
    def _():
        to_south.wait_send()
        to_north.wait_recv()

    @pl.when(jnp.logical_not(top))
    def _():
        to_north.wait_send()
        to_south.wait_recv()

    @pl.when(top)
    def _():
        own_fold.wait()
        for step in range(1, n_lon):
            fold_copy(step).wait_send()
        for step in range(1, n_lon):
            fold_arrival(step).wait_recv()


def exchange_and_ice(n_lon, n_lat, owned, state, depth, ivel, mass, strength, mask):
    anywhere = pl.BlockSpec(memory_space=pl.ANY)
    plane = pltpu.VMEM((LT, ROWS, 128), F32)
    plane_i = pltpu.VMEM((LT, ROWS, 128), I32)

    def body(*refs):
        exchange_kernel(n_lon, n_lat, *refs)

    return pl.pallas_call(
        body,
        name="exchange_and_ice",
        out_shape=(
            jax.ShapeDtypeStruct((ROWS, 128), F32),
            jax.ShapeDtypeStruct((ROWS, 128), F32),
            jax.ShapeDtypeStruct((16, COLS), F32),
            jax.ShapeDtypeStruct((16, COLS), F32),
            jax.ShapeDtypeStruct((n_lon, LT + 1, 8, 128), F32),
            jax.ShapeDtypeStruct((SLOTS, 2, TILE, TILE), F32),
            jax.ShapeDtypeStruct((SLOTS,), I32),
        ),
        in_specs=[pl.BlockSpec(memory_space=pltpu.SMEM)] + [anywhere] * 6,
        out_specs=(anywhere,) * 5
        + (pl.BlockSpec(memory_space=pltpu.VMEM), pl.BlockSpec(memory_space=pltpu.SMEM)),
        scratch_shapes=[
            plane_i,
            plane,
            plane,
            plane,
            plane,
            plane,
            plane,
            plane_i,
            pltpu.VMEM((2, LEV, ROWS, 128), F32),
            pltpu.VMEM((3, LEV, ROWS, 128), F32),
            pltpu.VMEM((2, LEV, 8, COLS), F32),
            pltpu.VMEM((3, LEV, 8, COLS), F32),
            pltpu.VMEM((ROWS, 128), F32),
            pltpu.VMEM((ROWS, 128), F32),
            pltpu.VMEM((16, COLS), F32),
            pltpu.VMEM((16, COLS), F32),
            pltpu.VMEM((LT + 1, 8, 128), F32),
            pltpu.VMEM((8, 128), I32),
            pltpu.VMEM((2, 8, 128), I32),
            pltpu.SMEM((2, 8, 128), I32),
            pltpu.VMEM((6, TILE, TILE), F32),
            pltpu.VMEM((6, NB, 8, 128), F32),
            pltpu.VMEM((5, NB, 8, 128), F32),
            pltpu.SemaphoreType.DMA((5,)),
            pltpu.SemaphoreType.DMA((6,)),
            pltpu.SemaphoreType.DMA((6,)),
            pltpu.SemaphoreType.DMA((n_lon,)),
            pltpu.SemaphoreType.DMA((n_lon,)),
            pltpu.SemaphoreType.DMA((2,)),
            pltpu.SemaphoreType.DMA((8,)),
        ],
        compiler_params=pltpu.CompilerParams(
            collective_id=0, has_side_effects=True, vmem_limit_bytes=40 * 2**20
        ),
    )(owned, state, depth, ivel, mass, strength, mask)


def recip(value):
    r = pl.reciprocal(value, approx=True)
    return r * (2.0 - value * r)


def face(open_depth, level, velocity):
    is_open = open_depth > level
    z = jnp.where(is_open, velocity * 0.25, 0.0)
    e = jnp.where(is_open, 0.125, 0.0)
    far = e - jnp.minimum(z, 0.0)
    return far, far + z


def ocean_kernel(
    n_lon,
    n_lat,
    partner,
    info,
    state,
    depth,
    vmix,
    ivel,
    he,
    hw,
    hs,
    hn,
    fold,
    res,
    out,
    out_ice,
    c_v,
    u_v,
    v_v,
    d_v,
    vm_v,
    o_v,
    ice_v,
    he_v,
    hw_v,
    hs_v,
    hn_v,
    fold_v,
    win,
    prev,
    in_sem,
    out_sem,
    sem,
):
    y = lax.axis_index("lat")
    top = y == n_lat - 1
    bottom = y == 0
    lane, row = iotas()
    lane16 = lax.broadcasted_iota(I32, (16, 128), 1)

    small = [
        pltpu.make_async_copy(he, he_v, sem.at[0]),
        pltpu.make_async_copy(hw, hw_v, sem.at[1]),
        pltpu.make_async_copy(hs, hs_v, sem.at[2]),
        pltpu.make_async_copy(hn, hn_v, sem.at[3]),
    ]
    get_fold = pltpu.make_async_copy(fold, fold_v, sem.at[4])
    get_ice = pltpu.make_async_copy(ivel, ice_v, sem.at[5])
    put_ice = pltpu.make_async_copy(ice_v, out_ice, sem.at[6])

    def fetch(i):
        rows = pl.ds(pl.multiple_of(i * 8, 8), 8)
        return [
            pltpu.make_async_copy(state.at[0:2, :, rows, :], c_v.at[:, :, rows, :], in_sem.at[0, i]),
            pltpu.make_async_copy(state.at[2, :, rows, :], u_v.at[:, rows, :], in_sem.at[1, i]),
            pltpu.make_async_copy(state.at[3, :, rows, :], v_v.at[:, rows, :], in_sem.at[2, i]),
            pltpu.make_async_copy(depth.at[rows, :], d_v.at[rows, :], in_sem.at[3, i]),
            pltpu.make_async_copy(vmix.at[:, rows, :], vm_v.at[:, rows, :], in_sem.at[4, i]),
        ]

    def put(i):
        rows = pl.ds(pl.multiple_of(i * 8, 8), 8)
        return pltpu.make_async_copy(o_v.at[:, :, rows, :], out.at[:, :, rows, :], out_sem.at[i])

    @pl.when(top)
    def _():
        get_fold.start()

    for c in small:
        c.start()

    def start_fetch(i, carry):
        for c in fetch(i):
            c.start()
        return carry

    lax.fori_loop(0, NB, start_fetch, 0)
    get_ice.start()
    for c in small:
        c.wait()

    @pl.when(top)
    def _():
        get_fold.wait()
        base = partner[COLS - 1]
        tile0 = lax.div(base, 128)
        shift = lax.rem(base, 128)
        for m in range(LT + 1):
            t = lax.rem(tile0 + m, n_lon * LT)
            dev = lax.div(t, LT)
            j = lax.rem(t, LT)
            win[m, 0:8, :] = fold_v[dev, j]
            win[m, 8:9, :] = fold_v[dev, LT, pl.ds(j, 1), :]
        back = lax.rem(128 - shift, 128)
        for m in range(LT):
            near = pltpu.roll(win[m], back, 1)
            far = pltpu.roll(win[m + 1], back, 1)
            value = jnp.where(lane16 < 128 - shift, near, far)
            for bit in (1, 2, 4, 8, 16, 32, 64):
                value = jnp.where(
                    (lane16 & bit) != 0, pltpu.roll(value, bit, 1), pltpu.roll(value, 128 - bit, 1)
                )
            at = (LT - 1 - m) * 128
            hn_v[:, at : at + 128] = value

    @pl.when(bottom)
    def _():
        hs_v[...] = jnp.zeros((16, COLS), F32)

    for t in range(2):
        for k in range(LEV):
            n = t * LEV + k
            c_v[t, k, ROWS : ROWS + 1, :] = hn_v[n : n + 1, :]
    d_v[ROWS : ROWS + 1, :] = hn_v[8:9, :].astype(I32)

    for c in fetch(0):
        c.wait()

    for j in range(LT):
        cols = slice(j * 128, j * 128 + 128)
        d_s = jnp.broadcast_to(hs_v[8:9, cols], (8, 128))
        open_s = jnp.minimum(d_v[0:8, cols].astype(F32), d_s)
        for k in range(LEV):
            far, near = face(open_s, k, jnp.broadcast_to(hs_v[9 + k : 10 + k, cols], (8, 128)))
            for t in range(2):
                n = t * LEV + k
                south = jnp.broadcast_to(hs_v[n : n + 1, cols], (8, 128))
                prev[n, :, cols] = c_v[t, k, 0:8, cols] * far - south * near

    def block(i, carry):
        @pl.when(i < NB - 1)
        def _():
            for c in fetch(i + 1):
                c.wait()

        rows = pl.ds(pl.multiple_of(i * 8, 8), 8)
        rows_n = pl.ds(pl.multiple_of(i * 8 + 8, 8), 8)

        west_pack = hw_v[rows, :]
        east_pack = he_v[rows, :]
        d0 = d_v[rows, 0:128].astype(F32)
        open_w = jnp.minimum(d0, pltpu.roll(west_pack, 128 - 8, 1))
        west = [None] * 8
        for k in range(LEV):
            far, near = face(open_w, k, pltpu.roll(west_pack, 128 - 9 - k, 1))
            for t in range(2):
                n = t * LEV + k
                c_w = west_pack if n == 0 else pltpu.roll(west_pack, 128 - n, 1)
                west[n] = c_v[t, k, rows, 0:128] * far - c_w * near

        c_own = [c_v[n // LEV, n % LEV, rows, 0:128] for n in range(8)]
        c_roll = [pltpu.roll(value, 127, 1) for value in c_own]
        d_own = d0
        d_roll = pltpu.roll(d0, 127, 1)
        for j in range(LT):
            cols = slice(j * 128, j * 128 + 128)
            nxt = slice(j * 128 + 128, j * 128 + 256)
            if j < LT - 1:
                d_next = d_v[rows, nxt].astype(F32)
                d_next_roll = pltpu.roll(d_next, 127, 1)
                c_next = [c_v[n // LEV, n % LEV, rows, nxt] for n in range(8)]
                c_next_roll = [pltpu.roll(value, 127, 1) for value in c_next]
            else:
                d_next = None
                d_next_roll = pltpu.roll(east_pack, 127 - 8, 1)
                c_next = None
                c_next_roll = [pltpu.roll(east_pack, 127 - n, 1) for n in range(8)]
            d_e = jnp.where(lane == 127, d_next_roll, d_roll)
            d_n = jnp.where(
                row == 7,
                pltpu.roll(d_v[rows_n, cols].astype(F32), 7, 0),
                pltpu.roll(d_own, 7, 0),
            )
            open_e = jnp.minimum(d_own, d_e)
            open_n = jnp.minimum(d_own, d_n)
            rhs = [None] * 8
            for k in range(LEV):
                e_far, e_near = face(open_e, k, u_v[k, rows, cols])
                n_far, n_near = face(open_n, k, v_v[k, rows, cols])
                for t in range(2):
                    n = t * LEV + k
                    c = c_own[n]
                    c_e = jnp.where(lane == 127, c_next_roll[n], c_roll[n])
                    c_n = jnp.where(
                        row == 7, pltpu.roll(c_v[t, k, rows_n, cols], 7, 0), pltpu.roll(c, 7, 0)
                    )
                    east = c_e * e_far - c * e_near
                    north = c_n * n_far - c * n_near
                    east_roll = pltpu.roll(east, 1, 1)
                    north_roll = pltpu.roll(north, 1, 0)
                    from_west = jnp.where(lane == 0, west[n], east_roll)
                    from_south = jnp.where(row == 0, prev[n, :, cols], north_roll)
                    west[n] = east_roll
                    prev[n, :, cols] = north_roll
                    rhs[n] = c + ((east - from_west) + (north - from_south))
            g = [jnp.where(d_own > k, vm_v[k, rows, cols] * 0.25, 0.0) for k in range(LEV)]
            i0 = recip((1.0 + g[0]) + g[1])
            u0 = g[1] * i0
            i1 = recip((1.0 + g[1]) + g[2] - g[1] * u0)
            u1 = g[2] * i1
            i2 = recip((1.0 + g[2]) + g[3] - g[2] * u1)
            u2 = g[3] * i2
            i3 = recip((1.0 + g[3]) - g[3] * u2)
            for t in range(2):
                f = rhs[t * LEV : t * LEV + LEV]
                r0 = f[0] * i0
                r1 = (f[1] + g[1] * r0) * i1
                r2 = (f[2] + g[2] * r1) * i2
                x3 = (f[3] + g[3] * r2) * i3
                x2 = r2 + u2 * x3
                x1 = r1 + u1 * x2
                x0 = r0 + u0 * x1
                for k, value in enumerate((x0, x1, x2, x3)):
                    o_v[t, k, rows, cols] = value
            c_own, c_roll, d_own, d_roll = c_next, c_next_roll, d_next, d_next_roll
        put(i).start()
        return carry

    lax.fori_loop(0, NB // 2, block, 0)

    get_ice.wait()
    for slot in range(SLOTS):
        pos = info[slot]

        @pl.when(pos >= 0)
        def _(slot=slot, pos=pos):
            at = pl.multiple_of(jnp.clip(pos, 0, LT - 1) * 128, 128)
            copy = pltpu.make_async_copy(
                res.at[slot], ice_v.at[:, :, pl.ds(at, 128)], sem.at[7 + slot]
            )
            copy.start()

    for slot in range(SLOTS):
        pos = info[slot]

        @pl.when(pos >= 0)
        def _(slot=slot, pos=pos):
            at = pl.multiple_of(jnp.clip(pos, 0, LT - 1) * 128, 128)
            copy = pltpu.make_async_copy(
                res.at[slot], ice_v.at[:, :, pl.ds(at, 128)], sem.at[7 + slot]
            )
            copy.wait()

    put_ice.start()
    lax.fori_loop(NB // 2, NB, block, 0)

    def drain(i, carry):
        put(i).wait()
        return carry

    lax.fori_loop(0, NB, drain, 0)
    put_ice.wait()


def ocean(n_lon, n_lat, partner, info, state, depth, vmix, ivel, he, hw, hs, hn, fold, res):
    anywhere = pl.BlockSpec(memory_space=pl.ANY)
    smem = pl.BlockSpec(memory_space=pltpu.SMEM)

    def body(*refs):
        ocean_kernel(n_lon, n_lat, *refs)

    return pl.pallas_call(
        body,
        name="ocean",
        out_shape=(
            jax.ShapeDtypeStruct((2, LEV, ROWS, COLS), F32),
            jax.ShapeDtypeStruct((2, ROWS, COLS), F32),
        ),
        in_specs=[smem, smem] + [anywhere] * 10,
        out_specs=(anywhere, anywhere),
        scratch_shapes=[
            pltpu.VMEM((2, LEV, ROWS + 8, COLS), F32),
            pltpu.VMEM((LEV, ROWS, COLS), F32),
            pltpu.VMEM((LEV, ROWS, COLS), F32),
            pltpu.VMEM((ROWS + 8, COLS), I32),
            pltpu.VMEM((LEV, ROWS, COLS), F32),
            pltpu.VMEM((2, LEV, ROWS, COLS), F32),
            pltpu.VMEM((2, ROWS, COLS), F32),
            pltpu.VMEM((ROWS, 128), F32),
            pltpu.VMEM((ROWS, 128), F32),
            pltpu.VMEM((16, COLS), F32),
            pltpu.VMEM((16, COLS), F32),
            pltpu.VMEM((n_lon, LT + 1, 8, 128), F32),
            pltpu.VMEM((LT + 1, 16, 128), F32),
            pltpu.VMEM((8, 8, COLS), F32),
            pltpu.SemaphoreType.DMA((5, NB)),
            pltpu.SemaphoreType.DMA((NB,)),
            pltpu.SemaphoreType.DMA((7 + SLOTS,)),
        ],
        compiler_params=pltpu.CompilerParams(vmem_limit_bytes=48 * 2**20),
    )(partner, info, state, depth, vmix, ivel, he, hw, hs, hn, fold, res)


def on_device(state, depth, vmix, partner, ivel, mass, strength, mask, owned):
    n_lon, n_lat = lax.axis_size("lon"), lax.axis_size("lat")
    he, hw, hs, hn, fold, res, info = exchange_and_ice(
        n_lon, n_lat, owned, state, depth, ivel, mass, strength, mask
    )
    return ocean(n_lon, n_lat, partner, info, state, depth, vmix, ivel, he, hw, hs, hn, fold, res)


def solution(mesh):
    return jax.shard_map(
        on_device,
        mesh=mesh,
        in_specs=(
            P(None, None, "lat", "lon"),
            P("lat", "lon"),
            P(None, "lat", "lon"),
            P("lon"),
            P(None, "lat", "lon"),
            P("lat", "lon"),
            P("lat", "lon"),
            P("lat", "lon"),
            P("lat", "lon", None),
        ),
        out_specs=(P(None, None, "lat", "lon"), P(None, "lat", "lon")),
        check_vma=False,
    )
```

profile of v0, /device:TPU:70, one launch (start us, length us, event | category | flops | bytes accessed | tf_op | source)
XLA Modules:
  0.0 50.5 jit_solution(5418694018610516227)
XLA Ops:
  0.6 0.0 copy-start
  0.6 3.4 %copy-done = f32[4,4,128,1024]{3,2,1,0:T(8,128)S(1)} copy-done((f32[4,4,128,1024]{3,2,1,0:T(8,128)S(1)}, f32[4,4,128,1024]{3,2,1,0:T(8,128)}, u32[]{:S(2)}) %copy-start) | copy-done | bytes 8388632
  4.0 0.0 copy-start.1
  4.0 1.2 %copy-done.1 = f32[2,128,1024]{2,1,0:T(8,128)S(1)} copy-done((f32[2,128,1024]{2,1,0:T(8,128)S(1)}, f32[2,128,1024]{2,1,0:T(8,128)}, u32[]{:S(2)}) %copy-start.1) | copy-done | bytes 1048600
  5.2 0.0 copy-start.4
  5.2 1.0 %copy-done.4 = s32[128,1024]{1,0:T(8,128)S(1)} copy-done((s32[128,1024]{1,0:T(8,128)S(1)}, s32[128,1024]{1,0:T(8,128)}, u32[]{:S(2)}) %copy-start.4) | copy-done | bytes 524312
  6.3 0.0 copy-start.5
  6.3 1.0 %copy-done.5 = f32[128,1024]{1,0:T(8,128)S(1)} copy-done((f32[128,1024]{1,0:T(8,128)S(1)}, f32[128,1024]{1,0:T(8,128)}, u32[]{:S(2)}) %copy-start.5) | copy-done | bytes 524312
  7.3 0.0 copy-start.6
  7.3 1.0 %copy-done.6 = f32[128,1024]{1,0:T(8,128)S(1)} copy-done((f32[128,1024]{1,0:T(8,128)S(1)}, f32[128,1024]{1,0:T(8,128)}, u32[]{:S(2)}) %copy-start.6) | copy-done | bytes 524312
  8.4 0.0 copy-start.7
  8.4 1.0 %copy-done.7 = s32[128,1024]{1,0:T(8,128)S(1)} copy-done((s32[128,1024]{1,0:T(8,128)S(1)}, s32[128,1024]{1,0:T(8,128)}, u32[]{:S(2)}) %copy-start.7) | copy-done | bytes 524312
  9.4 0.0 copy-start.9
  9.4 0.7 %copy-done.9 = s32[1,1,3]{2,1,0:T(1,128)S(1)} copy-done((s32[1,1,3]{2,1,0:T(1,128)S(1)}, s32[1,1,3]{2,1,0:T(1,128)}, u32[]{:S(2)}) %copy-start.9) | copy-done | bytes 36
  10.1 0.0 copy-start.2
  10.1 0.0 copy-start.3
  10.1 0.0 copy-start.8
  10.1 29.0 %exchange_and_ice.1 = (f32[128,128]{1,0:T(8,128)S(1)}, f32[128,128]{1,0:T(8,128)S(1)}, f32[16,1024]{1,0:T(8,128)S(1)}, f32[16,1024]{1,0:T(8,128)S(1)}, f32[16,9,...) custom-call(s32[1,1,3]{2,1,0:T(1,128)S(1)} %copy-done.9, f32[4,4,128,1024]{3,2,1,0:T(8,128)S(1)} %copy-done, ...), custom_call_target="tpu_custom_call" | custom-call | tf_op jit(solution)/shard_map/exchange_and_ice/pallas_call | solution.py:396
  39.1 0.0 copy-done.2
  39.1 0.0 copy-done.3
  39.1 0.0 copy-done.8
  39.2 11.3 %ocean.1 = (f32[2,4,128,1024]{3,2,1,0:T(8,128)}, f32[2,128,1024]{2,1,0:T(8,128)}) custom-call(s32[1024]{0:T(1024)S(1)} %copy-done.8, s32[3]{0:T(128)S(1)} %get-tuple-element.9.refs_1_, f32[4,4,128,1024]{3,2,1,0:T(8,128)} %refs_2_.3, s32[128,1024]{1,0:T(8,128)S(1)} %copy-done.4, f32[4,128,1024]{2,1,0:T(8,128)S(1)} %copy-done.3, ...), custom_call_target="tpu_custom_call" | custom-call | tf_op jit(solution)/shard_map/ocean/pallas_call | solution.py:724
Async XLA Ops:
  0.6 3.4 %copy-start = (f32[4,4,128,1024]{3,2,1,0:T(8,128)S(1)}, f32[4,4,128,1024]{3,2,1,0:T(8,128)}, u32[]{:S(2)}) copy-start(f32[4,4,128,1024]{3,2,1,0:T(8,128)} %refs_2_.3) | copy-start | bytes 25165828
  4.0 1.2 %copy-start.1 = (f32[2,128,1024]{2,1,0:T(8,128)S(1)}, f32[2,128,1024]{2,1,0:T(8,128)}, u32[]{:S(2)}) copy-start(f32[2,128,1024]{2,1,0:T(8,128)} %refs_5_.3) | copy-start | bytes 3145732
  5.2 1.0 %copy-start.4 = (s32[128,1024]{1,0:T(8,128)S(1)}, s32[128,1024]{1,0:T(8,128)}, u32[]{:S(2)}) copy-start(s32[128,1024]{1,0:T(8,128)} %refs_3_.3) | copy-start | bytes 1572868
  6.3 1.0 %copy-start.5 = (f32[128,1024]{1,0:T(8,128)S(1)}, f32[128,1024]{1,0:T(8,128)}, u32[]{:S(2)}) copy-start(f32[128,1024]{1,0:T(8,128)} %refs_4_.2) | copy-start | bytes 1572868
  7.3 1.0 %copy-start.6 = (f32[128,1024]{1,0:T(8,128)S(1)}, f32[128,1024]{1,0:T(8,128)}, u32[]{:S(2)}) copy-start(f32[128,1024]{1,0:T(8,128)} %refs_5_.2) | copy-start | bytes 1572868
  8.4 1.0 %copy-start.7 = (s32[128,1024]{1,0:T(8,128)S(1)}, s32[128,1024]{1,0:T(8,128)}, u32[]{:S(2)}) copy-start(s32[128,1024]{1,0:T(8,128)} %refs_6_.1) | copy-start | bytes 1572868
  9.4 0.7 %copy-start.9 = (s32[1,1,3]{2,1,0:T(1,128)S(1)}, s32[1,1,3]{2,1,0:T(1,128)}, u32[]{:S(2)}) copy-start(s32[1,1,3]{2,1,0:T(1,128)} %refs_0_.2) | copy-start | bytes 40
  10.1 29.1 %copy-start.2 = (f32[2,128,1024]{2,1,0:T(8,128)S(1)}, f32[2,128,1024]{2,1,0:T(8,128)}, u32[]{:S(2)}) copy-start(f32[2,128,1024]{2,1,0:T(8,128)} %refs_5_.3) | copy-start | bytes 3145732
  10.1 29.1 %copy-start.3 = (f32[4,128,1024]{2,1,0:T(8,128)S(1)}, f32[4,128,1024]{2,1,0:T(8,128)}, u32[]{:S(2)}) copy-start(f32[4,128,1024]{2,1,0:T(8,128)} %refs_4_.3) | copy-start | bytes 6291460
  10.1 29.1 %copy-start.8 = (s32[1024]{0:T(1024)S(1)}, s32[1024]{0:T(1024)}, u32[]{:S(2)}) copy-start(s32[1024]{0:T(1024)} %refs_0_.3) | copy-start | bytes 12292
where the time goes:
time: 51.3 us; the launch traced here: 50.5 us
  Pallas kernels  40.4 us (79%)
  local copies, waits for them, and re-layouts  9.43 us (18%)
  between operations  0.68 us (1%)
    pallas_call x1, Pallas kernels, exchange_and_ice(): pl.pallas_call(body, name='exchange_and_ice', out_shape=(jax.ShapeDtypeSt...  29 us
    pallas_call x1, Pallas kernels, ocean(): pl.pallas_call(body, name='ocean', out_shape=(jax.ShapeDtypeStruct((2, LE...  11.3 us
    unnamed x20, local copies, waits for them, and re-layouts  9.43 us

commit v1 on v0

v1 whole, which is shorter than its diff:
```python
import jax
import jax.numpy as jnp
from jax import lax
from jax.experimental import pallas as pl
from jax.experimental.pallas import tpu as pltpu
from jax.sharding import PartitionSpec as P

MESH = pl.DeviceIdType.MESH
LEV = 4
TILE = 128
ROWS = 128
COLS = 1024
LT = COLS // TILE
SLOTS = 3
SUBCYCLES = 32
NB = ROWS // 8
F32 = jnp.float32
I32 = jnp.int32


def iotas():
    lane = lax.broadcasted_iota(I32, (8, 128), 1)
    row = lax.broadcasted_iota(I32, (8, 128), 0)
    return lane, row


def ice_tiles(places, planes, con, st, rolled, res_ref):
    lane, row = iotas()
    not_first, not_last = lane != 0, lane != 127
    tiles = range(len(places))
    ue_v, un_v, mass_v, str_v, mask_v, depth_v, uo_v, vo_v = planes
    zeros = jnp.zeros((8, 128), F32)

    def at(k):
        return slice(k * 8, k * 8 + 8)

    def north(value):
        return jnp.where(row == 7, 0.0, pltpu.roll(value, 7, 0))

    def south(value):
        return jnp.where(row == 0, 0.0, pltpu.roll(value, 1, 0))

    def keep_east(t, f, k, value):
        pltpu.store(rolled.at[t, f, at(k), :], pltpu.roll(value, 127, 1), mask=not_last)

    def keep_west(t, f, k, value):
        pltpu.store(rolled.at[t, f, at(k), :], pltpu.roll(value, 1, 1), mask=not_first)

    for t in tiles:
        pos = places[t]
        for b in range(NB):
            rows = slice(b * 8, b * 8 + 8)
            spread = pl.ds((b % 2) * 64 + b // 2, 8, stride=8)
            mass, strength = mass_v[pos, rows, :], str_v[pos, rows, :]
            ice = jnp.logical_and(mask_v[pos, rows, :] > 0, depth_v[pos, rows, :] > 0)
            mass = jnp.where(ice, mass, 0.0)
            strength = jnp.where(ice, strength, 0.0)
            inertia = mass * 2.0
            diag = inertia + 1.0
            turn = mass * 0.5
            inv = 1.0 / (diag * diag + turn * turn)
            con[t, 0, spread, :] = inertia
            con[t, 1, spread, :] = diag * inv
            con[t, 2, spread, :] = turn * inv
            con[t, 3, spread, :] = strength * (1.0 / 12.0)
            con[t, 4, spread, :] = uo_v[pos, rows, :] * 0.5
            con[t, 5, spread, :] = vo_v[pos, rows, :] * 0.5
            st[t, 0, spread, :] = ue_v[pos, rows, :] * 0.5
            st[t, 1, spread, :] = un_v[pos, rows, :] * 0.5
            st[t, 2, spread, :] = strength * 0.25
    for t in tiles:
        for k in range(NB):
            for f in range(4):
                rolled[t, f, at(k), :] = zeros
    for t in tiles:
        for k in range(NB):
            p4 = st[t, 2, at(k), :]
            p_south = st[t, 2, at(k - 1), :] if k else south(st[t, 2, at(NB - 1), :])
            p_west = jnp.where(lane == 0, 0.0, pltpu.roll(p4, 1, 1))
            con[t, 4, at(k), :] = con[t, 4, at(k), :] - (p4 - p_west)
            con[t, 5, at(k), :] = con[t, 5, at(k), :] - (p4 - p_south)
            st[t, 3, at(k), :] = p4
            st[t, 4, at(k), :] = zeros
            keep_east(t, 0, k, st[t, 0, at(k), :])
            keep_east(t, 1, k, st[t, 1, at(k), :])

    keep = 1.0 / 1.5

    def stress(t, k):
        u, v = st[t, 0, at(k), :], st[t, 1, at(k), :]
        if k < NB - 1:
            un, vn = st[t, 0, at(k + 1), :], st[t, 1, at(k + 1), :]
        else:
            un, vn = north(st[t, 0, at(0), :]), north(st[t, 1, at(0), :])
        d1 = rolled[t, 0, at(k), :] - u
        d2 = vn - v
        h = (un - u) + (rolled[t, 1, at(k), :] - v)
        div = d1 + d2
        ten = d1 - d2
        p = div + div
        r = ten * 0.5
        q = con[t, 3, at(k), :] * lax.rsqrt((p * p + ten * ten) + (h * h + 0.25))
        sx = st[t, 2, at(k), :] * keep + q * (p + r)
        sy = st[t, 3, at(k), :] * keep + q * (p - r)
        sh = st[t, 4, at(k), :] * keep + q * h
        st[t, 2, at(k), :] = sx
        st[t, 3, at(k), :] = sy
        st[t, 4, at(k), :] = sh
        keep_west(t, 2, k, sx)
        keep_west(t, 3, k, sh)

    def momentum(t, k):
        u, v, sx, sy, sh = [st[t, f, at(k), :] for f in range(5)]
        if k:
            sy_s, sh_s = st[t, 3, at(k - 1), :], st[t, 4, at(k - 1), :]
        else:
            sy_s, sh_s = south(st[t, 3, at(NB - 1), :]), south(st[t, 4, at(NB - 1), :])
        inertia, al, be, kx, ky = [con[t, f, at(k), :] for f in (0, 1, 2, 4, 5)]
        rx = (inertia * u + kx) + ((sx - rolled[t, 2, at(k), :]) + (sh - sh_s))
        ry = (inertia * v + ky) + ((sh - rolled[t, 3, at(k), :]) + (sy - sy_s))
        u = al * rx + be * ry
        v = al * ry - be * rx
        st[t, 0, at(k), :] = u
        st[t, 1, at(k), :] = v
        keep_east(t, 0, k, u)
        keep_east(t, 1, k, v)

    def cycle(_, carry):
        for t in tiles:
            for k in range(NB):
                stress(t, k)
        for t in tiles:
            for k in range(NB):
                momentum(t, k)
        return carry

    lax.fori_loop(0, SUBCYCLES, cycle, 0, unroll=4)
    for t in tiles:
        for k in range(NB):
            res_ref[t, 0, pl.ds(k, 8, stride=NB), :] = st[t, 0, at(k), :] * 2.0
            res_ref[t, 1, pl.ds(k, 8, stride=NB), :] = st[t, 1, at(k), :] * 2.0


def exchange_kernel(
    n_lon,
    n_lat,
    owned_hbm,
    state,
    depth,
    ivel,
    mass,
    strength,
    mask,
    he,
    hw,
    hs,
    hn,
    fold,
    res,
    info,
    depth_v,
    uo_v,
    vo_v,
    ue_v,
    un_v,
    mass_v,
    str_v,
    mask_v,
    col_first,
    col_last,
    blk_first,
    blk_last,
    pack_first,
    pack_last,
    pack_n,
    pack_s,
    pack_f,
    my_list,
    lists,
    lists_s,
    con,
    st,
    rolled,
    load_sem,
    send_sem,
    recv_sem,
    fsend_sem,
    frecv_sem,
    local_sem,
    plane_sem,
    owned,
):
    x = lax.axis_index("lon")
    y = lax.axis_index("lat")
    lane, row = iotas()
    top = y == n_lat - 1
    bottom = y == 0

    def lon(step):
        return {"lon": lax.rem(x + step + n_lon, n_lon), "lat": y}

    def lat(step):
        return {"lon": x, "lat": y + step}

    get_owned = pltpu.make_async_copy(owned_hbm, owned, local_sem.at[2])
    get_owned.start()
    barrier = pltpu.get_barrier_semaphore()

    def greet(device):
        pl.semaphore_signal(barrier, inc=1, device_id=device, device_id_type=MESH)

    for step in (1, -1, 2, -2):
        greet(lon(step))

    @pl.when(top)
    def _():
        for step in range(3, n_lon - 2):
            greet(lon(step))

    @pl.when(jnp.logical_not(top))
    def _():
        greet(lat(1))

    @pl.when(jnp.logical_not(bottom))
    def _():
        greet(lat(-1))

    loads = [
        (state.at[0:2, :, :, pl.ds(0, 128)], col_first),
        (state.at[0:3, :, :, pl.ds(COLS - 128, 128)], col_last),
        (state.at[0:2, :, pl.ds(0, 8), :], blk_first),
        (state.at[0:2, :, pl.ds(ROWS - 8, 8), :], blk_last.at[0:2]),
        (state.at[3, :, pl.ds(ROWS - 8, 8), :], blk_last.at[2]),
    ]
    planes = [
        (depth, depth_v),
        (ivel.at[0], ue_v),
        (ivel.at[1], un_v),
        (mass, mass_v),
        (strength, str_v),
        (mask, mask_v),
        (state.at[2, 0], uo_v),
        (state.at[3, 0], vo_v),
    ]
    copies = [pltpu.make_async_copy(s, d, load_sem.at[i]) for i, (s, d) in enumerate(loads)]
    for i, (s, d) in enumerate(planes):
        if i == 1:
            for c in copies:
                c.start()
        for j in range(LT):
            pltpu.make_async_copy(s.at[:, j * 128 : j * 128 + 128], d.at[j], plane_sem.at[i]).start()

    def plane_wait(i):
        pltpu.make_async_copy(planes[i][1], planes[i][1], plane_sem.at[i]).wait()

    get_owned.wait()
    my_list[...] = jnp.where(
        lane == 0, owned[0, 0, 0], jnp.where(lane == 1, owned[0, 0, 1], owned[0, 0, 2])
    )

    @pl.when(jnp.logical_and(top, jnp.logical_not(bottom)))
    def _():
        pl.semaphore_wait(barrier, n_lon)

    @pl.when(jnp.logical_and(bottom, jnp.logical_not(top)))
    def _():
        pl.semaphore_wait(barrier, 5)

    @pl.when(jnp.logical_not(jnp.logical_or(bottom, top)))
    def _():
        pl.semaphore_wait(barrier, 6)

    def remote(src, dst, i, device):
        return pltpu.make_async_remote_copy(
            src_ref=src,
            dst_ref=dst,
            send_sem=send_sem.at[i],
            recv_sem=recv_sem.at[i],
            device_id=device,
            device_id_type=MESH,
        )

    list_1 = remote(my_list, lists.at[0], 0, lon(-1))
    list_2 = remote(my_list, lists.at[1], 1, lon(-2))
    to_west = remote(pack_first, he, 2, lon(-1))
    to_east = remote(pack_last, hw, 3, lon(1))
    to_south = remote(pack_n, hn, 4, lat(-1))
    to_north = remote(pack_s, hs, 5, lat(1))
    list_1.start()
    list_2.start()

    plane_wait(0)
    for c in copies:
        c.wait()

    for b in range(NB):
        rows = slice(b * 8, b * 8 + 8)
        first = jnp.zeros((8, 128), F32)
        last = jnp.zeros((8, 128), F32)
        for t in range(2):
            for k in range(LEV):
                n = t * LEV + k
                value = col_first[t, k, rows, :]
                first = jnp.where(lane == n, value if n == 0 else pltpu.roll(value, n, 1), first)
                last = jnp.where(lane == n, pltpu.roll(col_last[t, k, rows, :], n + 1, 1), last)
        d_first = depth_v[0, rows, :].astype(F32)
        d_last = depth_v[LT - 1, rows, :].astype(F32)
        first = jnp.where(lane == 8, pltpu.roll(d_first, 8, 1), first)
        last = jnp.where(lane == 8, pltpu.roll(d_last, 9, 1), last)
        for k in range(LEV):
            last = jnp.where(lane == 9 + k, pltpu.roll(col_last[2, k, rows, :], 10 + k, 1), last)
        pack_first[rows, :] = first
        pack_last[rows, :] = last

    pack_n[...] = jnp.zeros((16, COLS), F32)
    pack_s[...] = jnp.zeros((16, COLS), F32)
    for t in range(2):
        for k in range(LEV):
            n = t * LEV + k
            pack_n[n : n + 1, :] = blk_first[t, k, 0:1, :]
            pack_s[n : n + 1, :] = blk_last[t, k, 7:8, :]
    for k in range(LEV):
        pack_s[9 + k : 10 + k, :] = blk_last[2, k, 7:8, :]
    for j in range(LT):
        cols = slice(j * 128, j * 128 + 128)
        pack_n[8:9, cols] = depth_v[j, 0:8, :].astype(F32)[0:1, :]
        pack_s[8:9, cols] = depth_v[j, ROWS - 8 : ROWS, :].astype(F32)[7:8, :]
        pack_f[j] = pack_s[0:8, j * 128 : j * 128 + 128]
        pack_f[LT, j : j + 1, :] = pack_s[8:9, j * 128 : j * 128 + 128]

    to_west.start()
    to_east.start()

    @pl.when(jnp.logical_not(bottom))
    def _():
        to_south.start()

    @pl.when(jnp.logical_not(top))
    def _():
        to_north.start()

    def fold_copy(step):
        return pltpu.make_async_remote_copy(
            src_ref=pack_f,
            dst_ref=fold.at[x],
            send_sem=fsend_sem.at[step],
            recv_sem=frecv_sem.at[x],
            device_id=lon(step),
            device_id_type=MESH,
        )

    def fold_arrival(step):
        source = lax.rem(x - step + n_lon, n_lon)
        return pltpu.make_async_remote_copy(
            src_ref=pack_f,
            dst_ref=fold.at[source],
            send_sem=fsend_sem.at[step],
            recv_sem=frecv_sem.at[source],
            device_id=lon(step),
            device_id_type=MESH,
        )

    own_fold = pltpu.make_async_copy(pack_f, fold.at[x], local_sem.at[0])

    @pl.when(top)
    def _():
        own_fold.start()
        for step in range(1, n_lon):
            fold_copy(step).start()

    for i in range(1, len(planes)):
        plane_wait(i)

    list_1.wait_recv()
    list_2.wait_recv()
    to_smem = pltpu.make_async_copy(lists, lists_s, local_sem.at[1])
    to_smem.start()
    to_smem.wait()
    places = []
    for slot, column in enumerate((owned[0, 0, 0], lists_s[0, 0, 1], lists_s[1, 0, 2])):
        info[slot] = jnp.where(column >= 0, column - x * LT, -1)
        places.append(jnp.clip(column - x * LT, 0, LT - 1))
    ice_tiles(
        places, (ue_v, un_v, mass_v, str_v, mask_v, depth_v, uo_v, vo_v), con, st, rolled, res
    )

    list_1.wait_send()
    list_2.wait_send()
    to_west.wait()
    to_east.wait()

    @pl.when(jnp.logical_not(bottom))
    def _():
        to_south.wait_send()
        to_north.wait_recv()

    @pl.when(jnp.logical_not(top))
    def _():
        to_north.wait_send()
        to_south.wait_recv()

    @pl.when(top)
    def _():
        own_fold.wait()
        for step in range(1, n_lon):
            fold_copy(step).wait_send()
        for step in range(1, n_lon):
            fold_arrival(step).wait_recv()


def exchange_and_ice(n_lon, n_lat, owned, state, depth, ivel, mass, strength, mask):
    anywhere = pl.BlockSpec(memory_space=pl.ANY)
    plane = pltpu.VMEM((LT, ROWS, 128), F32)
    plane_i = pltpu.VMEM((LT, ROWS, 128), I32)

    def body(*refs):
        exchange_kernel(n_lon, n_lat, *refs)

    return pl.pallas_call(
        body,
        name="exchange_and_ice",
        out_shape=(
            jax.ShapeDtypeStruct((ROWS, 128), F32),
            jax.ShapeDtypeStruct((ROWS, 128), F32),
            jax.ShapeDtypeStruct((16, COLS), F32),
            jax.ShapeDtypeStruct((16, COLS), F32),
            jax.ShapeDtypeStruct((n_lon, LT + 1, 8, 128), F32),
            jax.ShapeDtypeStruct((SLOTS, 2, TILE, TILE), F32),
            jax.ShapeDtypeStruct((SLOTS,), I32),
        ),
        in_specs=[pl.BlockSpec(memory_space=pltpu.HBM)] * 7,
        out_specs=(anywhere,) * 5
        + (pl.BlockSpec(memory_space=pltpu.VMEM), pl.BlockSpec(memory_space=pltpu.SMEM)),
        scratch_shapes=[
            plane_i,
            plane,
            plane,
            plane,
            plane,
            plane,
            plane,
            plane_i,
            pltpu.VMEM((2, LEV, ROWS, 128), F32),
            pltpu.VMEM((3, LEV, ROWS, 128), F32),
            pltpu.VMEM((2, LEV, 8, COLS), F32),
            pltpu.VMEM((3, LEV, 8, COLS), F32),
            pltpu.VMEM((ROWS, 128), F32),
            pltpu.VMEM((ROWS, 128), F32),
            pltpu.VMEM((16, COLS), F32),
            pltpu.VMEM((16, COLS), F32),
            pltpu.VMEM((LT + 1, 8, 128), F32),
            pltpu.VMEM((8, 128), I32),
            pltpu.VMEM((2, 8, 128), I32),
            pltpu.SMEM((2, 8, 128), I32),
            pltpu.VMEM((SLOTS, 6, TILE, TILE), F32),
            pltpu.VMEM((SLOTS, 5, TILE, TILE), F32),
            pltpu.VMEM((SLOTS, 4, TILE, TILE), F32),
            pltpu.SemaphoreType.DMA((5,)),
            pltpu.SemaphoreType.DMA((6,)),
            pltpu.SemaphoreType.DMA((6,)),
            pltpu.SemaphoreType.DMA((n_lon,)),
            pltpu.SemaphoreType.DMA((n_lon,)),
            pltpu.SemaphoreType.DMA((3,)),
            pltpu.SemaphoreType.DMA((8,)),
            pltpu.SMEM((1, 1, SLOTS), I32),
        ],
        compiler_params=pltpu.CompilerParams(
            collective_id=0, has_side_effects=True, vmem_limit_bytes=16 * 2**20
        ),
    )(owned, state, depth, ivel, mass, strength, mask)


def recip(value):
    r = pltpu.reciprocal(value, approx=True)
    return r * (2.0 - value * r)


def face(open_depth, level, velocity):
    is_open = open_depth > level
    z = jnp.where(is_open, velocity * 0.25, 0.0)
    e = jnp.where(is_open, 0.125, 0.0)
    far = e - jnp.minimum(z, 0.0)
    return far, far + z


def ocean_kernel(
    n_lon,
    n_lat,
    partner,
    info,
    state,
    depth,
    vmix,
    ivel,
    he,
    hw,
    hs,
    hn,
    fold,
    res,
    out,
    out_ice,
    c_v,
    u_v,
    v_v,
    d_v,
    vm_v,
    o_v,
    ice_v,
    he_v,
    hw_v,
    hs_v,
    hn_v,
    fold_v,
    win,
    c_rolled,
    d_rolled,
    h_west,
    h_north,
    in_sem,
    out_sem,
    sem,
):
    y = lax.axis_index("lat")
    top = y == n_lat - 1
    bottom = y == 0
    lane, _ = iotas()
    lane16 = lax.broadcasted_iota(I32, (16, 128), 1)

    small = [
        pltpu.make_async_copy(he, he_v, sem.at[0]),
        pltpu.make_async_copy(hw, hw_v, sem.at[1]),
        pltpu.make_async_copy(hs, hs_v, sem.at[2]),
        pltpu.make_async_copy(hn, hn_v, sem.at[3]),
    ]
    get_fold = pltpu.make_async_copy(fold, fold_v, sem.at[4])
    get_ice = pltpu.make_async_copy(ivel, ice_v, sem.at[5])
    put_ice = pltpu.make_async_copy(ice_v, out_ice, sem.at[6])

    def fetch(j):
        cols = pl.ds(pl.multiple_of(j * 128, 128), 128)
        rows = pl.ds(0, ROWS)
        return [
            pltpu.make_async_copy(state.at[0:2, :, :, cols], c_v.at[j, :, :, rows, :], in_sem.at[0, j]),
            pltpu.make_async_copy(depth.at[:, cols], d_v.at[j, rows, :], in_sem.at[1, j]),
            pltpu.make_async_copy(state.at[2, :, :, cols], u_v.at[j], in_sem.at[2, j]),
            pltpu.make_async_copy(state.at[3, :, :, cols], v_v.at[j], in_sem.at[3, j]),
            pltpu.make_async_copy(vmix.at[:, :, cols], vm_v.at[j], in_sem.at[4, j]),
        ]

    def put(j):
        cols = pl.ds(pl.multiple_of(j * 128, 128), 128)
        return pltpu.make_async_copy(o_v.at[j], out.at[:, :, :, cols], out_sem.at[j])

    def patch(slot):
        at = pl.multiple_of(jnp.clip(info[slot], 0, LT - 1) * 128, 128)
        return pltpu.make_async_copy(res.at[slot], ice_v.at[:, :, pl.ds(at, 128)], sem.at[7 + slot])

    @pl.when(top)
    def _():
        get_fold.start()

    for c in small:
        c.start()
    for j in range(LT):
        for c in fetch(j):
            c.start()
    get_ice.start()
    for c in small:
        c.wait()

    @pl.when(top)
    def _():
        get_fold.wait()
        base = partner[COLS - 1]
        tile0 = lax.div(base, 128)
        shift = lax.rem(base, 128)
        for m in range(LT + 1):
            t = lax.rem(tile0 + m, n_lon * LT)
            dev = lax.div(t, LT)
            j = lax.rem(t, LT)
            win[m, 0:8, :] = fold_v[dev, j]
            win[m, 8:9, :] = fold_v[dev, LT, pl.ds(j, 1), :]
        back = lax.rem(128 - shift, 128)
        values = []
        for m in range(LT):
            near = pltpu.roll(win[m], back, 1)
            far = pltpu.roll(win[m + 1], back, 1)
            values.append(jnp.where(lane16 < 128 - shift, near, far))
        for bit in (1, 2, 4, 8, 16, 32, 64):
            odd = (lane16 & bit) != 0
            values = [
                jnp.where(odd, pltpu.roll(value, bit, 1), pltpu.roll(value, 128 - bit, 1))
                for value in values
            ]
        for m in range(LT):
            at = (LT - 1 - m) * 128
            hn_v[:, at : at + 128] = values[m]

    @pl.when(bottom)
    def _():
        hs_v[...] = jnp.zeros((16, COLS), F32)

    for j in range(LT):
        cols = slice(j * 128, j * 128 + 128)
        for n in range(8):
            c_v[j, n // LEV, n % LEV, ROWS : ROWS + 1, :] = hn_v[n : n + 1, cols]
        d_v[j, ROWS : ROWS + 1, :] = hn_v[8:9, cols].astype(I32)
    for b in range(NB):
        rows = slice(b * 8, b * 8 + 8)
        pack = he_v[rows, :]
        for n in range(8):
            c_v[LT, n // LEV, n % LEV, rows, :] = pack if n == 0 else pltpu.roll(pack, 128 - n, 1)
        d_v[LT, rows, :] = pltpu.roll(pack, 120, 1).astype(I32)

    for c in fetch(0):
        c.wait()

    for b in range(NB):
        rows = slice(b * 8, b * 8 + 8)
        pack = hw_v[rows, :]
        own = d_v[0, rows, :].astype(F32)
        d_rolled[rows, :] = pltpu.roll(own, 127, 1)
        open_w = jnp.minimum(own, pltpu.roll(pack, 120, 1))
        for k in range(LEV):
            far, near = face(open_w, k, pltpu.roll(pack, 119 - k, 1))
            for t in range(2):
                n = t * LEV + k
                c_w = pack if n == 0 else pltpu.roll(pack, 128 - n, 1)
                c = c_v[0, t, k, rows, :]
                h_west[n, rows, :] = c * far - c_w * near
                c_rolled[n, rows, :] = pltpu.roll(c, 127, 1)

    def column(j, carry):
        @pl.when(j < LT - 1)
        def _():
            for c in fetch(j + 1):
                c.wait()

        @pl.when(j == 2)
        def _():
            get_ice.wait()
            for slot in range(SLOTS):

                @pl.when(info[slot] >= 0)
                def _(slot=slot):
                    patch(slot).start()

        @pl.when(j == 4)
        def _():
            for slot in range(SLOTS):

                @pl.when(info[slot] >= 0)
                def _(slot=slot):
                    patch(slot).wait()

            put_ice.start()

        cols = pl.ds(pl.multiple_of(j * 128, 128), 128)
        own = jnp.broadcast_to(d_v[j, 0:8, :].astype(F32)[0:1, :], (8, 128))
        open_s = jnp.minimum(own, jnp.broadcast_to(hs_v[8:9, cols], (8, 128)))
        for k in range(LEV):
            far, near = face(open_s, k, jnp.broadcast_to(hs_v[9 + k : 10 + k, cols], (8, 128)))
            for t in range(2):
                n = t * LEV + k
                c_s = jnp.broadcast_to(hs_v[n : n + 1, cols], (8, 128))
                c = jnp.broadcast_to(c_v[j, t, k, 0:1, :], (8, 128))
                h_north[n, 0:8, :] = c * far - c_s * near

        for b in range(NB):
            rows = slice(b * 8, b * 8 + 8)
            ahead = slice(b * 8 + 1, b * 8 + 9)
            store = slice(b * 8 + 8, b * 8 + 16)
            behind = slice(b * 8 + 7, b * 8 + 15)
            own = d_v[j, rows, :].astype(F32)
            d_next = pltpu.roll(d_v[j + 1, rows, :].astype(F32), 127, 1)
            open_e = jnp.minimum(own, jnp.where(lane == 127, d_next, d_rolled[rows, :]))
            open_n = jnp.minimum(own, d_v[j, ahead, :].astype(F32))
            d_rolled[rows, :] = d_next
            rhs = [None] * 8
            for k in range(LEV):
                e_far, e_near = face(open_e, k, u_v[j, k, rows, :])
                n_far, n_near = face(open_n, k, v_v[j, k, rows, :])
                for t in range(2):
                    n = t * LEV + k
                    c = c_v[j, t, k, rows, :]
                    c_next = pltpu.roll(c_v[j + 1, t, k, rows, :], 127, 1)
                    c_e = jnp.where(lane == 127, c_next, c_rolled[n, rows, :])
                    c_rolled[n, rows, :] = c_next
                    east = c_e * e_far - c * e_near
                    north = c_v[j, t, k, ahead, :] * n_far - c * n_near
                    h_north[n, store, :] = north
                    east_rolled = pltpu.roll(east, 1, 1)
                    from_west = jnp.where(lane == 0, h_west[n, rows, :], east_rolled)
                    h_west[n, rows, :] = east_rolled
                    rhs[n] = c + ((east - from_west) + (north - h_north[n, behind, :]))
            g = [jnp.where(own > k, vm_v[j, k, rows, :] * 0.25, 0.0) for k in range(LEV)]
            i0 = recip((1.0 + g[0]) + g[1])
            u0 = g[1] * i0
            i1 = recip((1.0 + g[1]) + g[2] - g[1] * u0)
            u1 = g[2] * i1
            i2 = recip((1.0 + g[2]) + g[3] - g[2] * u1)
            u2 = g[3] * i2
            i3 = recip((1.0 + g[3]) - g[3] * u2)
            for t in range(2):
                f = rhs[t * LEV : t * LEV + LEV]
                r0 = f[0] * i0
                r1 = (f[1] + g[1] * r0) * i1
                r2 = (f[2] + g[2] * r1) * i2
                x3 = (f[3] + g[3] * r2) * i3
                x2 = r2 + u2 * x3
                x1 = r1 + u1 * x2
                x0 = r0 + u0 * x1
                for k, value in enumerate((x0, x1, x2, x3)):
                    o_v[j, t, k, rows, :] = value
        put(j).start()
        return carry

    lax.fori_loop(0, LT, column, 0)
    for j in range(LT):
        put(j).wait()
    put_ice.wait()


def ocean(n_lon, n_lat, partner, info, state, depth, vmix, ivel, he, hw, hs, hn, fold, res):
    anywhere = pl.BlockSpec(memory_space=pl.ANY)
    smem = pl.BlockSpec(memory_space=pltpu.SMEM)

    def body(*refs):
        ocean_kernel(n_lon, n_lat, *refs)

    return pl.pallas_call(
        body,
        name="ocean",
        out_shape=(
            jax.ShapeDtypeStruct((2, LEV, ROWS, COLS), F32),
            jax.ShapeDtypeStruct((2, ROWS, COLS), F32),
        ),
        in_specs=[smem, smem] + [anywhere] * 10,
        out_specs=(anywhere, anywhere),
        scratch_shapes=[
            pltpu.VMEM((LT + 1, 2, LEV, ROWS + 8, 128), F32),
            pltpu.VMEM((LT, LEV, ROWS, 128), F32),
            pltpu.VMEM((LT, LEV, ROWS, 128), F32),
            pltpu.VMEM((LT + 1, ROWS + 8, 128), I32),
            pltpu.VMEM((LT, LEV, ROWS, 128), F32),
            pltpu.VMEM((LT, 2, LEV, ROWS, 128), F32),
            pltpu.VMEM((2, ROWS, COLS), F32),
            pltpu.VMEM((ROWS, 128), F32),
            pltpu.VMEM((ROWS, 128), F32),
            pltpu.VMEM((16, COLS), F32),
            pltpu.VMEM((16, COLS), F32),
            pltpu.VMEM((n_lon, LT + 1, 8, 128), F32),
            pltpu.VMEM((LT + 1, 16, 128), F32),
            pltpu.VMEM((8, ROWS, 128), F32),
            pltpu.VMEM((ROWS, 128), F32),
            pltpu.VMEM((8, ROWS, 128), F32),
            pltpu.VMEM((8, ROWS + 8, 128), F32),
            pltpu.SemaphoreType.DMA((5, LT)),
            pltpu.SemaphoreType.DMA((LT,)),
            pltpu.SemaphoreType.DMA((7 + SLOTS,)),
        ],
        compiler_params=pltpu.CompilerParams(vmem_limit_bytes=28 * 2**20),
    )(partner, info, state, depth, vmix, ivel, he, hw, hs, hn, fold, res)


def on_device(state, depth, vmix, partner, ivel, mass, strength, mask, owned):
    n_lon, n_lat = lax.axis_size("lon"), lax.axis_size("lat")
    in_hbm = [
        pltpu.with_memory_space_constraint(value, pltpu.HBM)
        for value in (owned, state, depth, ivel, mass, strength, mask)
    ]
    he, hw, hs, hn, fold, res, info = exchange_and_ice(n_lon, n_lat, *in_hbm)
    depth = in_hbm[2]
    return ocean(n_lon, n_lat, partner, info, state, depth, vmix, ivel, he, hw, hs, hn, fold, res)


def solution(mesh):
    return jax.shard_map(
        on_device,
        mesh=mesh,
        in_specs=(
            P(None, None, "lat", "lon"),
            P("lat", "lon"),
            P(None, "lat", "lon"),
            P("lon"),
            P(None, "lat", "lon"),
            P("lat", "lon"),
            P("lat", "lon"),
            P("lat", "lon"),
            P("lat", "lon", None),
        ),
        out_specs=(P(None, None, "lat", "lon"), P(None, "lat", "lon")),
        check_vma=False,
    )
```

time: 51.3 us -> 35.3 us (0.69)
  local copies, waits for them, and re-layouts: 9.43 us -> 0.02 us
  Pallas kernels: 40.4 us -> 34.1 us
    unnamed x20 -> x8, local copies, waits for them, and re-layouts: 9.43 us -> 0.02 us
    pallas_call x1, Pallas kernels: 29 us -> 20.7 us  [exchange_and_ice(): pl.pallas_call(body, name='exchange_and_ice', out_shape=(jax.ShapeDtypeSt...]
    pallas_call x1, Pallas kernels: 11.3 us -> 13.4 us  [ocean(): pl.pallas_call(body, name='ocean', out_shape=(jax.ShapeDtypeStruct((2, LE...]
where the time goes in v1:
time: 35.3 us; the launch traced here: 34.8 us
  Pallas kernels  34.1 us (97%)
  between operations  0.7 us (2%)
    pallas_call x1, Pallas kernels, exchange_and_ice(): pl.pallas_call(body, name='exchange_and_ice', out_shape=(jax.ShapeDtypeSt...  20.7 us
    pallas_call x1, Pallas kernels, ocean(): pl.pallas_call(body, name='ocean', out_shape=(jax.ShapeDtypeStruct((2, LE...  13.4 us

profile of v1, /device:TPU:70, one launch (start us, length us, event | category | flops | bytes accessed | tf_op | source)
XLA Modules:
  0.0 34.8 jit_solution(8846498250069103798)
XLA Ops:
  0.6 0.0 copy-start.1
  0.6 0.0 copy-start
  0.7 0.0 copy-start.3
  0.7 0.0 copy-start.2
  0.7 20.7 %exchange_and_ice.1 = (f32[128,128]{1,0:T(8,128)S(1)}, f32[128,128]{1,0:T(8,128)S(1)}, f32[16,1024]{1,0:T(8,128)S(1)}, f32[16,1024]{1,0:T(8,128)S(1)}, f32[16,9,...) custom-call(s32[1,1,3]{2,1,0:T(1,128)} %refs_0_.2, f32[4,4,128,1024]{3,2,1,0:T(8,128)} %refs_2_.3, ...), custom_call_target="tpu_custom_call" | custom-call | tf_op jit(solution)/shard_map/exchange_and_ice/pallas_call | solution.py:419
  21.4 0.0 copy-done.1
  21.4 0.0 copy-done
  21.4 0.0 copy-done.3
  21.5 0.0 copy-done.2
  21.5 13.4 %ocean.1 = (f32[2,4,128,1024]{3,2,1,0:T(8,128)}, f32[2,128,1024]{2,1,0:T(8,128)}) custom-call(s32[1024]{0:T(1024)S(1)} %copy-done.3, s32[3]{0:T(128)S(1)} %get-tuple-element.9.refs_1_, f32[4,4,128,1024]{3,2,1,0:T(8,128)S(1)} %copy-done, s32[128,1024]{1,0:T(8,128)} %refs_3_.3, f32[4,128,1024]{2,1,0:T(8,128)S(1)} %copy-done.2, f32[2,128,1024]{2,1,0:T(8,128)S(1)} %copy-done.1, ...), custom_call_target="tpu_custom_call" | custom-call | tf_op jit(solution)/shard_map/ocean/pallas_call | solution.py:732
Async XLA Ops:
  0.6 20.8 %copy-start.1 = (f32[2,128,1024]{2,1,0:T(8,128)S(1)}, f32[2,128,1024]{2,1,0:T(8,128)}, u32[]{:S(2)}) copy-start(f32[2,128,1024]{2,1,0:T(8,128)} %refs_5_.3) | copy-start | bytes 3145732
  0.6 20.8 %copy-start = (f32[4,4,128,1024]{3,2,1,0:T(8,128)S(1)}, f32[4,4,128,1024]{3,2,1,0:T(8,128)}, u32[]{:S(2)}) copy-start(f32[4,4,128,1024]{3,2,1,0:T(8,128)} %refs_2_.3) | copy-start | bytes 25165828
  0.7 20.8 %copy-start.3 = (s32[1024]{0:T(1024)S(1)}, s32[1024]{0:T(1024)}, u32[]{:S(2)}) copy-start(s32[1024]{0:T(1024)} %refs_0_.3) | copy-start | bytes 12292
  0.7 20.8 %copy-start.2 = (f32[4,128,1024]{2,1,0:T(8,128)S(1)}, f32[4,128,1024]{2,1,0:T(8,128)}, u32[]{:S(2)}) copy-start(f32[4,128,1024]{2,1,0:T(8,128)} %refs_4_.3) | copy-start | bytes 6291460

commit v2 on v1

v2 whole, which is shorter than its diff:
```python
import jax
import jax.numpy as jnp
from jax import lax
from jax.experimental import pallas as pl
from jax.experimental.pallas import tpu as pltpu
from jax.sharding import PartitionSpec as P

MESH = pl.DeviceIdType.MESH
LEV = 4
TILE = 128
ROWS = 128
COLS = 1024
LT = COLS // TILE
SLOTS = 3
SUBCYCLES = 32
NB = ROWS // 8
F32 = jnp.float32
I32 = jnp.int32


def iotas():
    lane = lax.broadcasted_iota(I32, (8, 128), 1)
    row = lax.broadcasted_iota(I32, (8, 128), 0)
    return lane, row


def recip(value):
    r = pltpu.reciprocal(value, approx=True)
    return r * (2.0 - value * r)


def face(open_depth, level, velocity):
    is_open = open_depth > level
    z = jnp.where(is_open, velocity * 0.25, 0.0)
    e = jnp.where(is_open, 0.125, 0.0)
    far = e - jnp.minimum(z, 0.0)
    return far, far + z


def ice_tiles(places, planes, con, st, rolled, res_ref, hook):
    lane, row = iotas()
    not_first, not_last = lane != 0, lane != 127
    tiles = range(len(places))
    ue_v, un_v, mass_v, str_v, mask_v, depth_v, uo_v, vo_v = planes
    zeros = jnp.zeros((8, 128), F32)

    def at(k):
        return slice(k * 8, k * 8 + 8)

    def north(value):
        return jnp.where(row == 7, 0.0, pltpu.roll(value, 7, 0))

    def south(value):
        return jnp.where(row == 0, 0.0, pltpu.roll(value, 1, 0))

    def keep_east(t, f, k, value):
        pltpu.store(rolled.at[t, f, at(k), :], pltpu.roll(value, 127, 1), mask=not_last)

    def keep_west(t, f, k, value):
        pltpu.store(rolled.at[t, f, at(k), :], pltpu.roll(value, 1, 1), mask=not_first)

    for t in tiles:
        pos = places[t]
        for b in range(NB):
            rows = slice(b * 8, b * 8 + 8)
            spread = pl.ds((b % 2) * 64 + b // 2, 8, stride=8)
            mass, strength = mass_v[pos, rows, :], str_v[pos, rows, :]
            ice = jnp.logical_and(mask_v[pos, rows, :] > 0, depth_v[pos, rows, :] > 0)
            mass = jnp.where(ice, mass, 0.0)
            strength = jnp.where(ice, strength, 0.0)
            inertia = mass * 2.0
            diag = inertia + 1.0
            turn = mass * 0.5
            inv = 1.0 / (diag * diag + turn * turn)
            con[t, 0, spread, :] = inertia
            con[t, 1, spread, :] = diag * inv
            con[t, 2, spread, :] = turn * inv
            con[t, 3, spread, :] = strength * (1.0 / 12.0)
            con[t, 4, spread, :] = uo_v[pos, 0, rows, :] * 0.5
            con[t, 5, spread, :] = vo_v[pos, 0, rows, :] * 0.5
            st[t, 0, spread, :] = ue_v[pos, rows, :] * 0.5
            st[t, 1, spread, :] = un_v[pos, rows, :] * 0.5
            st[t, 2, spread, :] = strength * 0.25
    for t in tiles:
        for k in range(NB):
            for f in range(4):
                rolled[t, f, at(k), :] = zeros
    for t in tiles:
        for k in range(NB):
            p4 = st[t, 2, at(k), :]
            p_south = st[t, 2, at(k - 1), :] if k else south(st[t, 2, at(NB - 1), :])
            p_west = jnp.where(lane == 0, 0.0, pltpu.roll(p4, 1, 1))
            con[t, 4, at(k), :] = con[t, 4, at(k), :] - (p4 - p_west)
            con[t, 5, at(k), :] = con[t, 5, at(k), :] - (p4 - p_south)
            st[t, 3, at(k), :] = p4
            st[t, 4, at(k), :] = zeros
            keep_east(t, 0, k, st[t, 0, at(k), :])
            keep_east(t, 1, k, st[t, 1, at(k), :])

    keep = 1.0 / 1.5

    def stress(t, k):
        u, v = st[t, 0, at(k), :], st[t, 1, at(k), :]
        if k < NB - 1:
            un, vn = st[t, 0, at(k + 1), :], st[t, 1, at(k + 1), :]
        else:
            un, vn = north(st[t, 0, at(0), :]), north(st[t, 1, at(0), :])
        d1 = rolled[t, 0, at(k), :] - u
        d2 = vn - v
        h = (un - u) + (rolled[t, 1, at(k), :] - v)
        div = d1 + d2
        ten = d1 - d2
        p = div + div
        r = ten * 0.5
        q = con[t, 3, at(k), :] * lax.rsqrt((p * p + ten * ten) + (h * h + 0.25))
        sx = st[t, 2, at(k), :] * keep + q * (p + r)
        sy = st[t, 3, at(k), :] * keep + q * (p - r)
        sh = st[t, 4, at(k), :] * keep + q * h
        st[t, 2, at(k), :] = sx
        st[t, 3, at(k), :] = sy
        st[t, 4, at(k), :] = sh
        keep_west(t, 2, k, sx)
        keep_west(t, 3, k, sh)

    def momentum(t, k):
        u, v, sx, sy, sh = [st[t, f, at(k), :] for f in range(5)]
        if k:
            sy_s, sh_s = st[t, 3, at(k - 1), :], st[t, 4, at(k - 1), :]
        else:
            sy_s, sh_s = south(st[t, 3, at(NB - 1), :]), south(st[t, 4, at(NB - 1), :])
        inertia, al, be, kx, ky = [con[t, f, at(k), :] for f in (0, 1, 2, 4, 5)]
        rx = (inertia * u + kx) + ((sx - rolled[t, 2, at(k), :]) + (sh - sh_s))
        ry = (inertia * v + ky) + ((sh - rolled[t, 3, at(k), :]) + (sy - sy_s))
        u = al * rx + be * ry
        v = al * ry - be * rx
        st[t, 0, at(k), :] = u
        st[t, 1, at(k), :] = v
        keep_east(t, 0, k, u)
        keep_east(t, 1, k, v)

    def cycle(_, carry):
        for t in tiles:
            for k in range(NB):
                stress(t, k)
        for t in tiles:
            for k in range(NB):
                momentum(t, k)
        return carry

    def four(i, carry):
        hook(i)
        for _ in range(4):
            cycle(i, carry)
        return carry

    lax.fori_loop(0, SUBCYCLES // 4, four, 0)
    for t in tiles:
        for k in range(NB):
            res_ref[t, 0, pl.ds(k, 8, stride=NB), :] = st[t, 0, at(k), :] * 2.0
            res_ref[t, 1, pl.ds(k, 8, stride=NB), :] = st[t, 1, at(k), :] * 2.0


def exchange_kernel(
    n_lon,
    n_lat,
    owned_hbm,
    state,
    depth,
    ivel,
    mass,
    strength,
    mask,
    he,
    hw,
    hs,
    hn,
    own_first,
    own_last,
    own_n,
    own_s,
    fold,
    interim,
    res,
    info,
    c_v,
    u_v,
    v_v,
    d_v,
    ue_v,
    un_v,
    mass_v,
    str_v,
    mask_v,
    c_rolled,
    d_rolled,
    h_west,
    h_north,
    part,
    p_v,
    pack_first,
    pack_last,
    pack_n,
    pack_s,
    pack_f,
    my_list,
    lists,
    lists_s,
    owned,
    con,
    st,
    rolled,
    in_sem,
    plane_sem,
    p_sem,
    send_sem,
    recv_sem,
    fsend_sem,
    frecv_sem,
    local_sem,
):
    x = lax.axis_index("lon")
    y = lax.axis_index("lat")
    lane, row = iotas()
    is_last, not_last = lane == 127, lane != 127
    is_first, not_first = lane == 0, lane != 0
    top = y == n_lat - 1
    bottom = y == 0
    half = lax.rem(x, 2)
    chip = lax.div(x, 2)

    def lon(step):
        return {"lon": lax.rem(x + step + n_lon, n_lon), "lat": y}

    def lat(step):
        return {"lon": x, "lat": y + step}

    get_owned = pltpu.make_async_copy(owned_hbm, owned, local_sem.at[0])
    get_owned.start()
    barrier = pltpu.get_barrier_semaphore()

    def greet(device):
        pl.semaphore_signal(barrier, inc=1, device_id=device, device_id_type=MESH)

    for step in (1, -1, 2, -2):
        greet(lon(step))

    fold_extra = range(4, n_lon - 2, 2)

    @pl.when(top)
    def _():
        for step in fold_extra:
            greet(lon(step))

    @pl.when(jnp.logical_not(top))
    def _():
        greet(lat(1))

    @pl.when(jnp.logical_not(bottom))
    def _():
        greet(lat(-1))

    def barrier_wait():
        @pl.when(jnp.logical_and(top, jnp.logical_not(bottom)))
        def _():
            pl.semaphore_wait(barrier, 5 + len(fold_extra))

        @pl.when(jnp.logical_and(bottom, jnp.logical_not(top)))
        def _():
            pl.semaphore_wait(barrier, 5)

        @pl.when(jnp.logical_not(jnp.logical_or(bottom, top)))
        def _():
            pl.semaphore_wait(barrier, 6)

    def fetch(j):
        cols = pl.ds(pl.multiple_of(j * 128, 128), 128)
        rows = pl.ds(0, ROWS)
        return [
            pltpu.make_async_copy(state.at[0:2, :, :, cols], c_v.at[j, :, :, rows, :], in_sem.at[0, j]),
            pltpu.make_async_copy(depth.at[:, cols], d_v.at[j, rows, :], in_sem.at[1, j]),
            pltpu.make_async_copy(state.at[2, :, :, cols], u_v.at[j], in_sem.at[2, j]),
            pltpu.make_async_copy(state.at[3, :, :, cols], v_v.at[j], in_sem.at[3, j]),
        ]

    for j in range(LT):
        for c in fetch(j):
            c.start()
    planes = [(ivel.at[0], ue_v), (ivel.at[1], un_v), (mass, mass_v), (strength, str_v), (mask, mask_v)]
    for i, (src, dst) in enumerate(planes):
        for j in range(LT):
            pltpu.make_async_copy(
                src.at[:, j * 128 : j * 128 + 128], dst.at[j], plane_sem.at[i]
            ).start()

    get_owned.wait()
    my_list[...] = jnp.where(
        lane == 0, owned[0, 0, 0], jnp.where(lane == 1, owned[0, 0, 1], owned[0, 0, 2])
    )

    def remote(src, dst, i, device):
        return pltpu.make_async_remote_copy(
            src_ref=src,
            dst_ref=dst,
            send_sem=send_sem.at[i],
            recv_sem=recv_sem.at[i],
            device_id=device,
            device_id_type=MESH,
        )

    list_1 = remote(my_list, lists.at[0], 0, lon(-1))
    list_2 = remote(my_list, lists.at[1], 1, lon(-2))
    to_west = remote(pack_first, he, 2, lon(-1))
    to_east = remote(pack_last, hw, 3, lon(1))
    to_south = remote(pack_n, hn, 4, lat(-1))
    to_north = remote(pack_s, hs, 5, lat(1))

    zeros = jnp.zeros((8, 128), F32)
    beyond = slice(ROWS, ROWS + 8)
    for j in range(LT):
        d_v[j, beyond, :] = jnp.zeros((8, 128), I32)
        for n in range(8):
            c_v[j, n // LEV, n % LEV, beyond, :] = zeros
    for n in range(8):
        h_north[n, 0:8, :] = zeros
        for b in range(NB):
            h_west[0, n, b * 8 : b * 8 + 8, :] = zeros
    for c in fetch(0):
        c.wait()
    for b in range(NB):
        rows = slice(b * 8, b * 8 + 8)
        pltpu.store(
            d_rolled.at[0, rows, :], pltpu.roll(d_v[0, rows, :].astype(F32), 127, 1), mask=not_last
        )
        for n in range(8):
            value = pltpu.roll(c_v[0, n // LEV, n % LEV, rows, :], 127, 1)
            pltpu.store(c_rolled.at[0, n, rows, :], value, mask=not_last)

    def put(j):
        return pltpu.make_async_copy(p_v.at[j], interim.at[j], p_sem.at[j])

    def column(j, carry):
        @pl.when(j < LT - 1)
        def _():
            for c in fetch(j + 1):
                c.wait()

        @pl.when(j == 3)
        def _():
            barrier_wait()
            list_1.start()
            list_2.start()

        cur = lax.rem(j, 2)
        nxt = 1 - cur
        after = jnp.minimum(j + 1, LT - 1)
        inside = jnp.where(j < LT - 1, 1.0, 0.0)

        def roll_next(b):
            rows = slice(b * 8, b * 8 + 8)
            value = pltpu.roll(d_v[after, rows, :].astype(F32) * inside, 127, 1)
            pltpu.store(d_rolled.at[cur, rows, :], value, mask=is_last)
            pltpu.store(d_rolled.at[nxt, rows, :], value, mask=not_last)
            for n in range(8):
                value = pltpu.roll(c_v[after, n // LEV, n % LEV, rows, :], 127, 1)
                pltpu.store(c_rolled.at[cur, n, rows, :], value, mask=is_last)
                pltpu.store(c_rolled.at[nxt, n, rows, :], value, mask=not_last)

        def fluxes(b):
            rows = slice(b * 8, b * 8 + 8)
            ahead = slice(b * 8 + 1, b * 8 + 9)
            store = slice(b * 8 + 8, b * 8 + 16)
            behind = slice(b * 8 + 7, b * 8 + 15)
            own = d_v[j, rows, :].astype(F32)
            open_e = jnp.minimum(own, d_rolled[cur, rows, :])
            open_n = jnp.minimum(own, d_v[j, ahead, :].astype(F32))
            for k in range(LEV):
                e_far, e_near = face(open_e, k, u_v[j, k, rows, :])
                n_far, n_near = face(open_n, k, v_v[j, k, rows, :])
                for t in range(2):
                    n = t * LEV + k
                    c = c_v[j, t, k, rows, :]
                    east = c_rolled[cur, n, rows, :] * e_far - c * e_near
                    east_rolled = pltpu.roll(east, 1, 1)
                    pltpu.store(h_west.at[cur, n, rows, :], east_rolled, mask=not_first)
                    pltpu.store(h_west.at[nxt, n, rows, :], east_rolled, mask=is_first)
                    north = c_v[j, t, k, ahead, :] * n_far - c * n_near
                    h_north[n, store, :] = north
                    part[n, rows, :] = (c + east) + (north - h_north[n, behind, :])

        def finish(b):
            rows = slice(b * 8, b * 8 + 8)
            for n in range(8):
                p_v[j, n, rows, :] = part[n, rows, :] - h_west[cur, n, rows, :]

        for b in range(NB + 6):
            if b < NB:
                roll_next(b)
            if 0 <= b - 3 < NB:
                fluxes(b - 3)
            if 0 <= b - 6 < NB:
                finish(b - 6)
        put(j).start()
        return carry

    lax.fori_loop(0, LT, column, 0)

    for b in range(NB):
        rows = slice(b * 8, b * 8 + 8)
        d_first = jnp.broadcast_to(d_v[0, rows, :].astype(F32)[:, 0:1], (8, 128))
        d_last = jnp.broadcast_to(d_v[LT - 1, rows, :].astype(F32)[:, 127:128], (8, 128))
        first, last = d_first, d_last
        for n in range(8):
            t, k = n // LEV, n % LEV
            value = c_v[0, t, k, rows, :]
            first = jnp.where(lane == n, value if n == 0 else pltpu.roll(value, n, 1), first)
            last = jnp.where(lane == n, pltpu.roll(c_v[LT - 1, t, k, rows, :], n + 1, 1), last)
        for k in range(LEV):
            value = pltpu.roll(u_v[LT - 1, k, rows, :], 9 + k, 1)
            last = jnp.where(lane == 8 + k, value, last)
        last = jnp.where(jnp.logical_and(lane >= 12, lane < 16), pltpu.roll(last, 4, 1), last)
        pack_first[rows, :] = first
        pack_last[rows, :] = last
    for j in range(LT):
        cols = slice(j * 128, j * 128 + 128)
        d_n = d_v[j, 0:8, :].astype(F32)[0:1, :]
        d_s = d_v[j, ROWS - 8 : ROWS, :].astype(F32)[7:8, :]
        for n in range(8):
            t, k = n // LEV, n % LEV
            pack_n[n : n + 1, cols] = c_v[j, t, k, 0:1, :]
            pack_s[n : n + 1, cols] = c_v[j, t, k, ROWS - 1 : ROWS, :]
            pack_s[8 + n : 9 + n, cols] = v_v[j, k, ROWS - 1 : ROWS, :]
        pack_n[8:16, cols] = zeros
        pack_n[16:24, cols] = jnp.broadcast_to(d_n, (8, 128))
        pack_s[16:24, cols] = jnp.broadcast_to(d_s, (8, 128))
        pack_f[j] = pack_s[0:8, cols]
        pack_f[LT, j : j + 1, :] = d_s

    to_west.start()
    to_east.start()

    @pl.when(jnp.logical_not(bottom))
    def _():
        to_south.start()

    @pl.when(jnp.logical_not(top))
    def _():
        to_north.start()

    steps = range(1, n_lon // 2)

    def fold_copy(step):
        return pltpu.make_async_remote_copy(
            src_ref=pack_f,
            dst_ref=fold.at[half, chip],
            send_sem=fsend_sem.at[step],
            recv_sem=frecv_sem.at[chip],
            device_id=lon(2 * step),
            device_id_type=MESH,
        )

    def fold_arrival(step):
        source = lax.rem(chip - step + n_lon // 2, n_lon // 2)
        return pltpu.make_async_remote_copy(
            src_ref=pack_f,
            dst_ref=fold.at[half, source],
            send_sem=fsend_sem.at[step],
            recv_sem=frecv_sem.at[source],
            device_id=lon(2 * step),
            device_id_type=MESH,
        )

    def fold_sibling(which):
        return pltpu.make_async_remote_copy(
            src_ref=fold.at[which],
            dst_ref=fold.at[which],
            send_sem=fsend_sem.at[0],
            recv_sem=frecv_sem.at[n_lon // 2],
            device_id=lon(1 - 2 * half),
            device_id_type=MESH,
        )

    own_fold = pltpu.make_async_copy(pack_f, fold.at[half, chip], local_sem.at[1])

    @pl.when(top)
    def _():
        own_fold.start()
        for step in steps:
            fold_copy(step).start()

    own_packs = [
        pltpu.make_async_copy(src, dst, local_sem.at[3 + i])
        for i, (src, dst) in enumerate(
            ((pack_first, own_first), (pack_last, own_last), (pack_n, own_n), (pack_s, own_s))
        )
    ]
    for c in own_packs:
        c.start()
    for i, (_, dst) in enumerate(planes):
        pltpu.make_async_copy(dst, dst, plane_sem.at[i]).wait()
    list_1.wait_recv()
    list_2.wait_recv()
    to_smem = pltpu.make_async_copy(lists, lists_s, local_sem.at[2])
    to_smem.start()
    to_smem.wait()
    places = []
    for slot, column_id in enumerate((owned[0, 0, 0], lists_s[0, 0, 1], lists_s[1, 0, 2])):
        info[slot] = jnp.where(column_id >= 0, column_id - x * LT, -1)
        places.append(jnp.clip(column_id - x * LT, 0, LT - 1))

    def hook(i):
        @pl.when(jnp.logical_and(top, i == 5))
        def _():
            own_fold.wait()
            for step in steps:
                fold_arrival(step).wait_recv()
            fold_sibling(half).start()

    ice_tiles(
        places, (ue_v, un_v, mass_v, str_v, mask_v, d_v, u_v, v_v), con, st, rolled, res, hook
    )

    list_1.wait_send()
    list_2.wait_send()
    to_west.wait()
    to_east.wait()
    for c in own_packs:
        c.wait()
    for j in range(LT):
        put(j).wait()

    @pl.when(jnp.logical_not(bottom))
    def _():
        to_south.wait_send()
        to_north.wait_recv()

    @pl.when(jnp.logical_not(top))
    def _():
        to_north.wait_send()
        to_south.wait_recv()

    @pl.when(top)
    def _():
        for step in steps:
            fold_copy(step).wait_send()
        fold_sibling(half).wait_send()
        fold_sibling(1 - half).wait_recv()


def exchange_and_ice(n_lon, n_lat, owned, state, depth, ivel, mass, strength, mask):
    anywhere = pl.BlockSpec(memory_space=pl.ANY)
    plane = pltpu.VMEM((LT, ROWS, 128), F32)
    column = jax.ShapeDtypeStruct((ROWS, 128), F32)
    rows = jax.ShapeDtypeStruct((24, COLS), F32)

    def body(*refs):
        exchange_kernel(n_lon, n_lat, *refs)

    return pl.pallas_call(
        body,
        name="exchange_and_ice",
        out_shape=(
            column,
            column,
            rows,
            rows,
            column,
            column,
            rows,
            rows,
            jax.ShapeDtypeStruct((2, n_lon // 2, LT + 1, 8, 128), F32),
            jax.ShapeDtypeStruct((LT, 8, ROWS, 128), F32),
            jax.ShapeDtypeStruct((SLOTS, 2, TILE, TILE), F32),
            jax.ShapeDtypeStruct((SLOTS,), I32),
        ),
        in_specs=[pl.BlockSpec(memory_space=pltpu.HBM)] * 7,
        out_specs=(anywhere,) * 10
        + (pl.BlockSpec(memory_space=pltpu.VMEM), pl.BlockSpec(memory_space=pltpu.SMEM)),
        scratch_shapes=[
            pltpu.VMEM((LT, 2, LEV, ROWS + 8, 128), F32),
            pltpu.VMEM((LT, LEV, ROWS, 128), F32),
            pltpu.VMEM((LT, LEV, ROWS, 128), F32),
            pltpu.VMEM((LT, ROWS + 8, 128), I32),
            plane,
            plane,
            plane,
            plane,
            pltpu.VMEM((LT, ROWS, 128), I32),
            pltpu.VMEM((2, 8, ROWS, 128), F32),
            pltpu.VMEM((2, ROWS, 128), F32),
            pltpu.VMEM((2, 8, ROWS, 128), F32),
            pltpu.VMEM((8, ROWS + 8, 128), F32),
            pltpu.VMEM((8, ROWS, 128), F32),
            pltpu.VMEM((LT, 8, ROWS, 128), F32),
            pltpu.VMEM((ROWS, 128), F32),
            pltpu.VMEM((ROWS, 128), F32),
            pltpu.VMEM((24, COLS), F32),
            pltpu.VMEM((24, COLS), F32),
            pltpu.VMEM((LT + 1, 8, 128), F32),
            pltpu.VMEM((8, 128), I32),
            pltpu.VMEM((2, 8, 128), I32),
            pltpu.SMEM((2, 8, 128), I32),
            pltpu.SMEM((1, 1, SLOTS), I32),
            pltpu.VMEM((SLOTS, 6, TILE, TILE), F32),
            pltpu.VMEM((SLOTS, 5, TILE, TILE), F32),
            pltpu.VMEM((SLOTS, 4, TILE, TILE), F32),
            pltpu.SemaphoreType.DMA((4, LT)),
            pltpu.SemaphoreType.DMA((5,)),
            pltpu.SemaphoreType.DMA((LT,)),
            pltpu.SemaphoreType.DMA((6,)),
            pltpu.SemaphoreType.DMA((6,)),
            pltpu.SemaphoreType.DMA((n_lon // 2,)),
            pltpu.SemaphoreType.DMA((n_lon // 2 + 1,)),
            pltpu.SemaphoreType.DMA((7,)),
        ],
        compiler_params=pltpu.CompilerParams(
            collective_id=0, has_side_effects=True, vmem_limit_bytes=28 * 2**20
        ),
    )(owned, state, depth, ivel, mass, strength, mask)


def ocean_kernel(
    n_lon,
    n_lat,
    partner,
    info,
    interim,
    depth,
    vmix,
    ivel,
    he,
    hw,
    hs,
    hn,
    own_first,
    own_last,
    own_n,
    own_s,
    fold,
    res,
    out,
    out_ice,
    p_v,
    d_v,
    vm_v,
    o_v,
    ice_v,
    he_v,
    hw_v,
    hs_v,
    hn_v,
    first_v,
    last_v,
    n_v,
    s_v,
    fold_v,
    win,
    west_h,
    east_h,
    south_h,
    north_h,
    in_sem,
    out_sem,
    sem,
):
    y = lax.axis_index("lat")
    top = y == n_lat - 1
    bottom = y == 0
    lane, row = iotas()
    lane16 = lax.broadcasted_iota(I32, (16, 128), 1)

    small = [
        pltpu.make_async_copy(src, dst, sem.at[i])
        for i, (src, dst) in enumerate(
            (
                (he, he_v),
                (hw, hw_v),
                (hs, hs_v),
                (hn, hn_v),
                (own_first, first_v),
                (own_last, last_v),
                (own_n, n_v),
                (own_s, s_v),
            )
        )
    ]
    get_fold = pltpu.make_async_copy(fold, fold_v, sem.at[8])
    get_ice = pltpu.make_async_copy(ivel, ice_v, sem.at[9])
    put_ice = pltpu.make_async_copy(ice_v, out_ice, sem.at[10])

    def fetch(j):
        cols = slice(j * 128, j * 128 + 128)
        return [
            pltpu.make_async_copy(interim.at[j], p_v.at[j], in_sem.at[0, j]),
            pltpu.make_async_copy(depth.at[:, cols], d_v.at[j], in_sem.at[1, j]),
            pltpu.make_async_copy(vmix.at[:, :, cols], vm_v.at[j], in_sem.at[2, j]),
        ]

    def put(j):
        cols = slice(j * 128, j * 128 + 128)
        return pltpu.make_async_copy(o_v.at[j], out.at[:, :, :, cols], out_sem.at[j])

    def patch(slot):
        at = pl.multiple_of(jnp.clip(info[slot], 0, LT - 1) * 128, 128)
        return pltpu.make_async_copy(res.at[slot], ice_v.at[:, :, pl.ds(at, 128)], sem.at[11 + slot])

    @pl.when(top)
    def _():
        get_fold.start()

    for c in small:
        c.start()
    get_ice.start()
    for j in range(LT):
        for c in fetch(j):
            c.start()
    for c in small:
        c.wait()

    @pl.when(top)
    def _():
        get_fold.wait()
        base = partner[COLS - 1]
        tile0 = lax.div(base, 128)
        shift = lax.rem(base, 128)
        for m in range(LT + 1):
            t = lax.rem(tile0 + m, n_lon * LT)
            dev = lax.div(t, LT)
            j = lax.rem(t, LT)
            half, chip = lax.rem(dev, 2), lax.div(dev, 2)
            win[m, 0:8, :] = fold_v[half, chip, j]
            win[m, 8:9, :] = fold_v[half, chip, LT, pl.ds(j, 1), :]
        back = lax.rem(128 - shift, 128)
        values = []
        for m in range(LT):
            near = pltpu.roll(win[m], back, 1)
            far = pltpu.roll(win[m + 1], back, 1)
            values.append(jnp.where(lane16 < 128 - shift, near, far))
        for bit in (1, 2, 4, 8, 16, 32, 64):
            odd = (lane16 & bit) != 0
            values = [
                jnp.where(odd, pltpu.roll(value, bit, 1), pltpu.roll(value, 128 - bit, 1))
                for value in values
            ]
        for m in range(LT):
            at = (LT - 1 - m) * 128
            hn_v[0:8, at : at + 128] = values[m][0:8, :]
            hn_v[16:24, at : at + 128] = jnp.broadcast_to(values[m][8:9, :], (8, 128))

    @pl.when(bottom)
    def _():
        hs_v[...] = jnp.zeros((24, COLS), F32)

    level = (lane & 3).astype(F32)
    for b in range(NB):
        rows = slice(b * 8, b * 8 + 8)
        pack, own = hw_v[rows, :], first_v[rows, :]
        both = jnp.minimum(pltpu.roll(pack, 112, 1), pltpu.roll(own, 112, 1))
        far, near = face(both, level, pltpu.roll(pack, 120, 1))
        west_h[rows, :] = pack * near - own * far
        pack, own = he_v[rows, :], last_v[rows, :]
        both = jnp.minimum(pltpu.roll(pack, 112, 1), pltpu.roll(own, 112, 1))
        far, near = face(both, level, pltpu.roll(own, 120, 1))
        east_h[rows, :] = pack * far - own * near
    level = (row & 3).astype(F32)
    for j in range(LT):
        cols = slice(j * 128, j * 128 + 128)
        far, near = face(jnp.minimum(s_v[16:24, cols], hn_v[16:24, cols]), level, s_v[8:16, cols])
        north_h[:, cols] = hn_v[0:8, cols] * far - s_v[0:8, cols] * near
        far, near = face(jnp.minimum(n_v[16:24, cols], hs_v[16:24, cols]), level, hs_v[8:16, cols])
        south_h[:, cols] = hs_v[0:8, cols] * near - n_v[0:8, cols] * far

    def rhs(j, n, b):
        rows = slice(b * 8, b * 8 + 8)
        value = p_v[j, n, rows, :]
        if j == 0:
            west = west_h[rows, :] if n == 0 else pltpu.roll(west_h[rows, :], 128 - n, 1)
            value = value + jnp.where(lane == 0, west, 0.0)
        if j == LT - 1:
            value = value + jnp.where(lane == 127, pltpu.roll(east_h[rows, :], 127 - n, 1), 0.0)
        cols = slice(j * 128, j * 128 + 128)
        if b == 0:
            rim = jnp.broadcast_to(south_h[n : n + 1, cols], (8, 128))
            value = value + jnp.where(row == 0, rim, 0.0)
        if b == NB - 1:
            rim = jnp.broadcast_to(north_h[n : n + 1, cols], (8, 128))
            value = value + jnp.where(row == 7, rim, 0.0)
        return value

    for j in range(LT):
        for c in fetch(j):
            c.wait()
        if j == 2:
            get_ice.wait()
            for slot in range(SLOTS):

                @pl.when(info[slot] >= 0)
                def _(slot=slot):
                    patch(slot).start()

        if j == 4:
            for slot in range(SLOTS):

                @pl.when(info[slot] >= 0)
                def _(slot=slot):
                    patch(slot).wait()

            put_ice.start()
        for b in range(NB):
            rows = slice(b * 8, b * 8 + 8)
            own = d_v[j, rows, :]
            g = [jnp.where(own > k, vm_v[j, k, rows, :] * 0.25, 0.0) for k in range(LEV)]
            i0 = recip((1.0 + g[0]) + g[1])
            u0 = g[1] * i0
            i1 = recip((1.0 + g[1]) + g[2] - g[1] * u0)
            u1 = g[2] * i1
            i2 = recip((1.0 + g[2]) + g[3] - g[2] * u1)
            u2 = g[3] * i2
            i3 = recip((1.0 + g[3]) - g[3] * u2)
            for t in range(2):
                f = [rhs(j, t * LEV + k, b) for k in range(LEV)]
                r0 = f[0] * i0
                r1 = (f[1] + g[1] * r0) * i1
                r2 = (f[2] + g[2] * r1) * i2
                x3 = (f[3] + g[3] * r2) * i3
                x2 = r2 + u2 * x3
                x1 = r1 + u1 * x2
                x0 = r0 + u0 * x1
                for k, value in enumerate((x0, x1, x2, x3)):
                    o_v[j, t, k, rows, :] = value
        put(j).start()

    for j in range(LT):
        put(j).wait()
    put_ice.wait()


def ocean(n_lon, n_lat, *operands):
    anywhere = pl.BlockSpec(memory_space=pl.ANY)
    smem = pl.BlockSpec(memory_space=pltpu.SMEM)
    column = pltpu.VMEM((ROWS, 128), F32)
    rows = pltpu.VMEM((24, COLS), F32)

    def body(*refs):
        ocean_kernel(n_lon, n_lat, *refs)

    return pl.pallas_call(
        body,
        name="ocean",
        out_shape=(
            jax.ShapeDtypeStruct((2, LEV, ROWS, COLS), F32),
            jax.ShapeDtypeStruct((2, ROWS, COLS), F32),
        ),
        in_specs=[smem, smem] + [anywhere] * (len(operands) - 2),
        out_specs=(anywhere, anywhere),
        scratch_shapes=[
            pltpu.VMEM((LT, 8, ROWS, 128), F32),
            pltpu.VMEM((LT, ROWS, 128), I32),
            pltpu.VMEM((LT, LEV, ROWS, 128), F32),
            pltpu.VMEM((LT, 2, LEV, ROWS, 128), F32),
            pltpu.VMEM((2, ROWS, COLS), F32),
            column,
            column,
            rows,
            rows,
            column,
            column,
            rows,
            rows,
            pltpu.VMEM((2, n_lon // 2, LT + 1, 8, 128), F32),
            pltpu.VMEM((LT + 1, 16, 128), F32),
            column,
            column,
            pltpu.VMEM((8, COLS), F32),
            pltpu.VMEM((8, COLS), F32),
            pltpu.SemaphoreType.DMA((3, LT)),
            pltpu.SemaphoreType.DMA((LT,)),
            pltpu.SemaphoreType.DMA((11 + SLOTS,)),
        ],
        compiler_params=pltpu.CompilerParams(vmem_limit_bytes=20 * 2**20),
    )(*operands)


def on_device(state, depth, vmix, partner, ivel, mass, strength, mask, owned):
    n_lon, n_lat = lax.axis_size("lon"), lax.axis_size("lat")
    in_hbm = [
        pltpu.with_memory_space_constraint(value, pltpu.HBM)
        for value in (owned, state, depth, ivel, mass, strength, mask)
    ]
    *rims, interim, res, info = exchange_and_ice(n_lon, n_lat, *in_hbm)
    return ocean(n_lon, n_lat, partner, info, interim, depth, vmix, ivel, *rims, res)


def solution(mesh):
    return jax.shard_map(
        on_device,
        mesh=mesh,
        in_specs=(
            P(None, None, "lat", "lon"),
            P("lat", "lon"),
            P(None, "lat", "lon"),
            P("lon"),
            P(None, "lat", "lon"),
            P("lat", "lon"),
            P("lat", "lon"),
            P("lat", "lon"),
            P("lat", "lon", None),
        ),
        out_specs=(P(None, None, "lat", "lon"), P(None, "lat", "lon")),
        check_vma=False,
    )
```

time: 35.3 us -> 32.5 us (0.921); the launches traced: 34.8 us -> 32.4 us
  Pallas kernels: 34.1 us -> 31.7 us
    pallas_call x1, Pallas kernels: 13.4 us -> 6.21 us  [ocean(): pl.pallas_call(body, name='ocean', out_shape=(jax.ShapeDtypeStruct((2, LE...]
    pallas_call x1, Pallas kernels: 20.7 us -> 25.5 us  [exchange_and_ice(): pl.pallas_call(body, name='exchange_and_ice', out_shape=(column, column,...]
where the time goes in v2:
time: 32.5 us; the launch traced here: 32.4 us
  Pallas kernels  31.7 us (98%)
  between operations  0.7 us (2%)
    pallas_call x1, Pallas kernels, exchange_and_ice(): pl.pallas_call(body, name='exchange_and_ice', out_shape=(column, column,...  25.5 us
    pallas_call x1, Pallas kernels, ocean(): pl.pallas_call(body, name='ocean', out_shape=(jax.ShapeDtypeStruct((2, LE...  6.21 us

profile of v2, /device:TPU:70, one launch (start us, length us, event | category | flops | bytes accessed | tf_op | source)
XLA Modules:
  0.0 32.4 jit_solution(8984249121677639663)
XLA Ops:
  0.6 0.0 copy-start
  0.6 0.0 copy-start.1
  0.7 0.0 copy-start.3
  0.7 0.0 copy-start.2
  0.7 25.5 %exchange_and_ice.1 = (f32[128,128]{1,0:T(8,128)S(1)}, f32[128,128]{1,0:T(8,128)S(1)}, f32[24,1024]{1,0:T(8,128)S(1)}, f32[24,1024]{1,0:T(8,128)S(1)}, f32[128,1...) custom-call(s32[1,1,3]{2,1,0:T(1,128)} %refs_0_.2, ...), custom_call_target="tpu_custom_call" | custom-call | tf_op jit(solution)/shard_map/exchange_and_ice/pallas_call | solution.py:558
  26.2 0.0 copy-done
  26.2 0.0 copy-done.1
  26.2 0.0 copy-done.3
  26.2 0.0 copy-done.2
  26.2 6.2 %ocean.1 = (f32[2,4,128,1024]{3,2,1,0:T(8,128)}, f32[2,128,1024]{2,1,0:T(8,128)}) custom-call(s32[1024]{0:T(1024)S(1)} %copy-done.3, s32[3]{0:T(128)S(1)} %get-tuple-element.14.refs_1_, f32[8,8,128,128]{3,2,1,0:T(8,128)S(1)} %get-tuple-element.15.refs_2_, s32[128,1024]{1,0:T(8,128)S(1)} %copy-done.1, f32[4,128,1024]{2,1,0:T(8,128)S(1)} %copy-done.2, ...), custom_call_target="tpu_custom_call" | custom-call | tf_op jit(solution)/shard_map/ocean/pallas_call | solution.py:846
Async XLA Ops:
  0.6 25.5 %copy-start = (f32[2,128,1024]{2,1,0:T(8,128)S(1)}, f32[2,128,1024]{2,1,0:T(8,128)}, u32[]{:S(2)}) copy-start(f32[2,128,1024]{2,1,0:T(8,128)} %refs_5_.3) | copy-start | bytes 3145732
  0.6 25.5 %copy-start.1 = (s32[128,1024]{1,0:T(8,128)S(1)}, s32[128,1024]{1,0:T(8,128)}, u32[]{:S(2)}) copy-start(s32[128,1024]{1,0:T(8,128)} %refs_3_.3) | copy-start | bytes 1572868
  0.7 25.5 %copy-start.3 = (s32[1024]{0:T(1024)S(1)}, s32[1024]{0:T(1024)}, u32[]{:S(2)}) copy-start(s32[1024]{0:T(1024)} %refs_0_.3) | copy-start | bytes 12292
  0.7 25.5 %copy-start.2 = (f32[4,128,1024]{2,1,0:T(8,128)S(1)}, f32[4,128,1024]{2,1,0:T(8,128)}, u32[]{:S(2)}) copy-start(f32[4,128,1024]{2,1,0:T(8,128)} %refs_4_.3) | copy-start | bytes 6291460

commit v3 on v2

--- a/solution.py
+++ b/solution.py
@@ -170,6 +170,7 @@
     mass,
     strength,
     mask,
+    vmix,
     he,
     hw,
     hs,
@@ -180,6 +181,9 @@
     own_s,
     fold,
     interim,
+    vmix_out,
+    depth_out,
+    ivel_out,
     res,
     info,
     c_v,
@@ -191,12 +195,14 @@
     mass_v,
     str_v,
     mask_v,
+    blk_first,
+    blk_last,
+    d_rim,
     c_rolled,
     d_rolled,
     h_west,
     h_north,
     part,
-    p_v,
     pack_first,
     pack_last,
     pack_n,
@@ -211,12 +217,13 @@
     rolled,
     in_sem,
     plane_sem,
-    p_sem,
     send_sem,
     recv_sem,
     fsend_sem,
     frecv_sem,
     local_sem,
+    rim_sem,
+    out_sem,
 ):
     x = lax.axis_index("lon")
     y = lax.axis_index("lat")
@@ -282,6 +289,15 @@
             pltpu.make_async_copy(state.at[3, :, :, cols], v_v.at[j], in_sem.at[3, j]),
         ]
 
+    rims = [
+        pltpu.make_async_copy(state.at[0:2, :, pl.ds(0, 8), :], blk_first, rim_sem.at[0]),
+        pltpu.make_async_copy(state.at[0:2, :, pl.ds(ROWS - 8, 8), :], blk_last.at[0:2], rim_sem.at[1]),
+        pltpu.make_async_copy(state.at[3, :, pl.ds(ROWS - 8, 8), :], blk_last.at[2], rim_sem.at[2]),
+        pltpu.make_async_copy(depth.at[pl.ds(0, 8), :], d_rim.at[0], rim_sem.at[3]),
+        pltpu.make_async_copy(depth.at[pl.ds(ROWS - 8, 8), :], d_rim.at[1], rim_sem.at[4]),
+    ]
+    for c in rims:
+        c.start()
     for j in range(LT):
         for c in fetch(j):
             c.start()
@@ -292,6 +308,13 @@
                 src.at[:, j * 128 : j * 128 + 128], dst.at[j], plane_sem.at[i]
             ).start()
 
+    passed = [pltpu.make_async_copy(ivel, ivel_out, out_sem.at[LT])] + [
+        pltpu.make_async_copy(vmix.at[:, :, j * 128 : j * 128 + 128], vmix_out.at[j], out_sem.at[j])
+        for j in range(LT)
+    ]
+    for c in passed:
+        c.start()
+
     get_owned.wait()
     my_list[...] = jnp.where(
         lane == 0, owned[0, 0, 0], jnp.where(lane == 1, owned[0, 0, 1], owned[0, 0, 2])
@@ -309,6 +332,7 @@
 
     list_1 = remote(my_list, lists.at[0], 0, lon(-1))
     list_2 = remote(my_list, lists.at[1], 1, lon(-2))
+    to_smem = pltpu.make_async_copy(lists, lists_s, local_sem.at[2])
     to_west = remote(pack_first, he, 2, lon(-1))
     to_east = remote(pack_last, hw, 3, lon(1))
     to_south = remote(pack_n, hn, 4, lat(-1))
@@ -324,6 +348,58 @@
         h_north[n, 0:8, :] = zeros
         for b in range(NB):
             h_west[0, n, b * 8 : b * 8 + 8, :] = zeros
+    for c in rims:
+        c.wait()
+    for j in range(LT):
+        cols = slice(j * 128, j * 128 + 128)
+        d_n = d_rim[0, :, cols].astype(F32)[0:1, :]
+        d_s = d_rim[1, :, cols].astype(F32)[7:8, :]
+        for n in range(8):
+            t, k = n // LEV, n % LEV
+            pack_n[n : n + 1, cols] = blk_first[t, k, 0:1, cols]
+            pack_s[n : n + 1, cols] = blk_last[t, k, 7:8, cols]
+            pack_s[8 + n : 9 + n, cols] = blk_last[2, k, 7:8, cols]
+        pack_n[8:16, cols] = zeros
+        pack_n[16:24, cols] = jnp.broadcast_to(d_n, (8, 128))
+        pack_s[16:24, cols] = jnp.broadcast_to(d_s, (8, 128))
+        pack_f[j] = pack_s[0:8, cols]
+        pack_f[LT, j : j + 1, :] = d_s
+
+    steps = range(1, n_lon // 2)
+
+    def fold_copy(step):
+        return pltpu.make_async_remote_copy(
+            src_ref=pack_f,
+            dst_ref=fold.at[half, chip],
+            send_sem=fsend_sem.at[step],
+            recv_sem=frecv_sem.at[chip],
+            device_id=lon(2 * step),
+            device_id_type=MESH,
+        )
+
+    def fold_arrival(step):
+        source = lax.rem(chip - step + n_lon // 2, n_lon // 2)
+        return pltpu.make_async_remote_copy(
+            src_ref=pack_f,
+            dst_ref=fold.at[half, source],
+            send_sem=fsend_sem.at[step],
+            recv_sem=frecv_sem.at[source],
+            device_id=lon(2 * step),
+            device_id_type=MESH,
+        )
+
+    def fold_sibling(which):
+        return pltpu.make_async_remote_copy(
+            src_ref=fold.at[which],
+            dst_ref=fold.at[which],
+            send_sem=fsend_sem.at[0],
+            recv_sem=frecv_sem.at[n_lon // 2],
+            device_id=lon(1 - 2 * half),
+            device_id_type=MESH,
+        )
+
+    own_fold = pltpu.make_async_copy(pack_f, fold.at[half, chip], local_sem.at[1])
+
     for c in fetch(0):
         c.wait()
     for b in range(NB):
@@ -335,20 +411,37 @@
             value = pltpu.roll(c_v[0, n // LEV, n % LEV, rows, :], 127, 1)
             pltpu.store(c_rolled.at[0, n, rows, :], value, mask=not_last)
 
-    def put(j):
-        return pltpu.make_async_copy(p_v.at[j], interim.at[j], p_sem.at[j])
-
     def column(j, carry):
         @pl.when(j < LT - 1)
         def _():
             for c in fetch(j + 1):
                 c.wait()
 
-        @pl.when(j == 3)
+        @pl.when(j == 2)
         def _():
             barrier_wait()
             list_1.start()
             list_2.start()
+
+            @pl.when(jnp.logical_not(bottom))
+            def _():
+                to_south.start()
+
+            @pl.when(jnp.logical_not(top))
+            def _():
+                to_north.start()
+
+            @pl.when(top)
+            def _():
+                own_fold.start()
+                for step in steps:
+                    fold_copy(step).start()
+
+        @pl.when(j == LT - 1)
+        def _():
+            list_1.wait_recv()
+            list_2.wait_recv()
+            to_smem.start()
 
         cur = lax.rem(j, 2)
         nxt = 1 - cur
@@ -390,7 +483,7 @@
         def finish(b):
             rows = slice(b * 8, b * 8 + 8)
             for n in range(8):
-                p_v[j, n, rows, :] = part[n, rows, :] - h_west[cur, n, rows, :]
+                interim[j, n, rows, :] = part[n, rows, :] - h_west[cur, n, rows, :]
 
         for b in range(NB + 6):
             if b < NB:
@@ -399,7 +492,6 @@
                 fluxes(b - 3)
             if 0 <= b - 6 < NB:
                 finish(b - 6)
-        put(j).start()
         return carry
 
     lax.fori_loop(0, LT, column, 0)
@@ -420,72 +512,8 @@
         last = jnp.where(jnp.logical_and(lane >= 12, lane < 16), pltpu.roll(last, 4, 1), last)
         pack_first[rows, :] = first
         pack_last[rows, :] = last
-    for j in range(LT):
-        cols = slice(j * 128, j * 128 + 128)
-        d_n = d_v[j, 0:8, :].astype(F32)[0:1, :]
-        d_s = d_v[j, ROWS - 8 : ROWS, :].astype(F32)[7:8, :]
-        for n in range(8):
-            t, k = n // LEV, n % LEV
-            pack_n[n : n + 1, cols] = c_v[j, t, k, 0:1, :]
-            pack_s[n : n + 1, cols] = c_v[j, t, k, ROWS - 1 : ROWS, :]
-            pack_s[8 + n : 9 + n, cols] = v_v[j, k, ROWS - 1 : ROWS, :]
-        pack_n[8:16, cols] = zeros
-        pack_n[16:24, cols] = jnp.broadcast_to(d_n, (8, 128))
-        pack_s[16:24, cols] = jnp.broadcast_to(d_s, (8, 128))
-        pack_f[j] = pack_s[0:8, cols]
-        pack_f[LT, j : j + 1, :] = d_s
-
     to_west.start()
     to_east.start()
-
-    @pl.when(jnp.logical_not(bottom))
-    def _():
-        to_south.start()
-
-    @pl.when(jnp.logical_not(top))
-    def _():
-        to_north.start()
-
-    steps = range(1, n_lon // 2)
-
-    def fold_copy(step):
-        return pltpu.make_async_remote_copy(
-            src_ref=pack_f,
-            dst_ref=fold.at[half, chip],
-            send_sem=fsend_sem.at[step],
-            recv_sem=frecv_sem.at[chip],
-            device_id=lon(2 * step),
-            device_id_type=MESH,
-        )
-
-    def fold_arrival(step):
-        source = lax.rem(chip - step + n_lon // 2, n_lon // 2)
-        return pltpu.make_async_remote_copy(
-            src_ref=pack_f,
-            dst_ref=fold.at[half, source],
-            send_sem=fsend_sem.at[step],
-            recv_sem=frecv_sem.at[source],
-            device_id=lon(2 * step),
-            device_id_type=MESH,
-        )
-
-    def fold_sibling(which):
-        return pltpu.make_async_remote_copy(
-            src_ref=fold.at[which],
-            dst_ref=fold.at[which],
-            send_sem=fsend_sem.at[0],
-            recv_sem=frecv_sem.at[n_lon // 2],
-            device_id=lon(1 - 2 * half),
-            device_id_type=MESH,
-        )
-
-    own_fold = pltpu.make_async_copy(pack_f, fold.at[half, chip], local_sem.at[1])
-
-    @pl.when(top)
-    def _():
-        own_fold.start()
-        for step in steps:
-            fold_copy(step).start()
 
     own_packs = [
         pltpu.make_async_copy(src, dst, local_sem.at[3 + i])
@@ -493,14 +521,12 @@
             ((pack_first, own_first), (pack_last, own_last), (pack_n, own_n), (pack_s, own_s))
         )
     ]
+    give_depth = pltpu.make_async_copy(d_v.at[:, pl.ds(0, ROWS), :], depth_out, out_sem.at[LT + 1])
+    give_depth.start()
     for c in own_packs:
         c.start()
     for i, (_, dst) in enumerate(planes):
         pltpu.make_async_copy(dst, dst, plane_sem.at[i]).wait()
-    list_1.wait_recv()
-    list_2.wait_recv()
-    to_smem = pltpu.make_async_copy(lists, lists_s, local_sem.at[2])
-    to_smem.start()
     to_smem.wait()
     places = []
     for slot, column_id in enumerate((owned[0, 0, 0], lists_s[0, 0, 1], lists_s[1, 0, 2])):
@@ -508,7 +534,7 @@
         places.append(jnp.clip(column_id - x * LT, 0, LT - 1))
 
     def hook(i):
-        @pl.when(jnp.logical_and(top, i == 5))
+        @pl.when(jnp.logical_and(top, i == 2))
         def _():
             own_fold.wait()
             for step in steps:
@@ -523,11 +549,9 @@
     list_2.wait_send()
     to_west.wait()
     to_east.wait()
-    for c in own_packs:
+    give_depth.wait()
+    for c in own_packs + passed:
         c.wait()
-    for j in range(LT):
-        put(j).wait()
-
     @pl.when(jnp.logical_not(bottom))
     def _():
         to_south.wait_send()
@@ -546,8 +570,9 @@
         fold_sibling(1 - half).wait_recv()
 
 
-def exchange_and_ice(n_lon, n_lat, owned, state, depth, ivel, mass, strength, mask):
+def exchange_and_ice(n_lon, n_lat, *operands):
     anywhere = pl.BlockSpec(memory_space=pl.ANY)
+    inside = pl.BlockSpec(memory_space=pltpu.VMEM)
     plane = pltpu.VMEM((LT, ROWS, 128), F32)
     column = jax.ShapeDtypeStruct((ROWS, 128), F32)
     rows = jax.ShapeDtypeStruct((24, COLS), F32)
@@ -569,12 +594,17 @@
             rows,
             jax.ShapeDtypeStruct((2, n_lon // 2, LT + 1, 8, 128), F32),
             jax.ShapeDtypeStruct((LT, 8, ROWS, 128), F32),
+            jax.ShapeDtypeStruct((LT, LEV, ROWS, 128), F32),
+            jax.ShapeDtypeStruct((LT, ROWS, 128), I32),
+            jax.ShapeDtypeStruct((2, ROWS, COLS), F32),
             jax.ShapeDtypeStruct((SLOTS, 2, TILE, TILE), F32),
             jax.ShapeDtypeStruct((SLOTS,), I32),
         ),
-        in_specs=[pl.BlockSpec(memory_space=pltpu.HBM)] * 7,
-        out_specs=(anywhere,) * 10
-        + (pl.BlockSpec(memory_space=pltpu.VMEM), pl.BlockSpec(memory_space=pltpu.SMEM)),
+        in_specs=[pl.BlockSpec(memory_space=pltpu.HBM)] * 8,
+        out_specs=(anywhere,) * 9
+        + (inside,)
+        + (anywhere,) * 3
+        + (inside, pl.BlockSpec(memory_space=pltpu.SMEM)),
         scratch_shapes=[
             pltpu.VMEM((LT, 2, LEV, ROWS + 8, 128), F32),
             pltpu.VMEM((LT, LEV, ROWS, 128), F32),
@@ -585,12 +615,14 @@
             plane,
             plane,
             pltpu.VMEM((LT, ROWS, 128), I32),
+            pltpu.VMEM((2, LEV, 8, COLS), F32),
+            pltpu.VMEM((3, LEV, 8, COLS), F32),
+            pltpu.VMEM((2, 8, COLS), I32),
             pltpu.VMEM((2, 8, ROWS, 128), F32),
             pltpu.VMEM((2, ROWS, 128), F32),
             pltpu.VMEM((2, 8, ROWS, 128), F32),
             pltpu.VMEM((8, ROWS + 8, 128), F32),
             pltpu.VMEM((8, ROWS, 128), F32),
-            pltpu.VMEM((LT, 8, ROWS, 128), F32),
             pltpu.VMEM((ROWS, 128), F32),
             pltpu.VMEM((ROWS, 128), F32),
             pltpu.VMEM((24, COLS), F32),
@@ -605,17 +637,18 @@
             pltpu.VMEM((SLOTS, 4, TILE, TILE), F32),
             pltpu.SemaphoreType.DMA((4, LT)),
             pltpu.SemaphoreType.DMA((5,)),
-            pltpu.SemaphoreType.DMA((LT,)),
             pltpu.SemaphoreType.DMA((6,)),
             pltpu.SemaphoreType.DMA((6,)),
             pltpu.SemaphoreType.DMA((n_lon // 2,)),
             pltpu.SemaphoreType.DMA((n_lon // 2 + 1,)),
             pltpu.SemaphoreType.DMA((7,)),
+            pltpu.SemaphoreType.DMA((5,)),
+            pltpu.SemaphoreType.DMA((LT + 2,)),
         ],
         compiler_params=pltpu.CompilerParams(
-            collective_id=0, has_side_effects=True, vmem_limit_bytes=28 * 2**20
+            collective_id=0, has_side_effects=True, vmem_limit_bytes=22 * 2**20
         ),
-    )(owned, state, depth, ivel, mass, strength, mask)
+    )(*operands)
 
 
 def ocean_kernel(
@@ -623,9 +656,9 @@
     n_lat,
     partner,
     info,
-    interim,
-    depth,
-    vmix,
+    p_v,
+    vm_v,
+    d_v,
     ivel,
     he,
     hw,
@@ -639,26 +672,14 @@
     res,
     out,
     out_ice,
-    p_v,
-    d_v,
-    vm_v,
     o_v,
-    ice_v,
-    he_v,
-    hw_v,
     hs_v,
     hn_v,
-    first_v,
-    last_v,
-    n_v,
-    s_v,
-    fold_v,
     win,
     west_h,
     east_h,
     south_h,
     north_h,
-    in_sem,
     out_sem,
     sem,
 ):
@@ -668,32 +689,7 @@
     lane, row = iotas()
     lane16 = lax.broadcasted_iota(I32, (16, 128), 1)
 
-    small = [
-        pltpu.make_async_copy(src, dst, sem.at[i])
-        for i, (src, dst) in enumerate(
-            (
-                (he, he_v),
-                (hw, hw_v),
-                (hs, hs_v),
-                (hn, hn_v),
-                (own_first, first_v),
-                (own_last, last_v),
-                (own_n, n_v),
-                (own_s, s_v),
-            )
-        )
-    ]
-    get_fold = pltpu.make_async_copy(fold, fold_v, sem.at[8])
-    get_ice = pltpu.make_async_copy(ivel, ice_v, sem.at[9])
-    put_ice = pltpu.make_async_copy(ice_v, out_ice, sem.at[10])
-
-    def fetch(j):
-        cols = slice(j * 128, j * 128 + 128)
-        return [
-            pltpu.make_async_copy(interim.at[j], p_v.at[j], in_sem.at[0, j]),
-            pltpu.make_async_copy(depth.at[:, cols], d_v.at[j], in_sem.at[1, j]),
-            pltpu.make_async_copy(vmix.at[:, :, cols], vm_v.at[j], in_sem.at[2, j]),
-        ]
+    put_ice = pltpu.make_async_copy(ivel, out_ice, sem.at[0])
 
     def put(j):
         cols = slice(j * 128, j * 128 + 128)
@@ -701,24 +697,14 @@
 
     def patch(slot):
         at = pl.multiple_of(jnp.clip(info[slot], 0, LT - 1) * 128, 128)
-        return pltpu.make_async_copy(res.at[slot], ice_v.at[:, :, pl.ds(at, 128)], sem.at[11 + slot])
+        return pltpu.make_async_copy(res.at[slot], out_ice.at[:, :, pl.ds(at, 128)], sem.at[1 + slot])
+
+    put_ice.start()
+    hn_v[...] = hn[...]
+    hs_v[...] = hs[...]
 
     @pl.when(top)
     def _():
-        get_fold.start()
-
-    for c in small:
-        c.start()
-    get_ice.start()
-    for j in range(LT):
-        for c in fetch(j):
-            c.start()
-    for c in small:
-        c.wait()
-
-    @pl.when(top)
-    def _():
-        get_fold.wait()
         base = partner[COLS - 1]
         tile0 = lax.div(base, 128)
         shift = lax.rem(base, 128)
@@ -727,8 +713,8 @@
             dev = lax.div(t, LT)
             j = lax.rem(t, LT)
             half, chip = lax.rem(dev, 2), lax.div(dev, 2)
-            win[m, 0:8, :] = fold_v[half, chip, j]
-            win[m, 8:9, :] = fold_v[half, chip, LT, pl.ds(j, 1), :]
+            win[m, 0:8, :] = fold[half, chip, j]
+            win[m, 8:9, :] = fold[half, chip, LT, pl.ds(j, 1), :]
         back = lax.rem(128 - shift, 128)
         values = []
         for m in range(LT):
@@ -753,21 +739,21 @@
     level = (lane & 3).astype(F32)
     for b in range(NB):
         rows = slice(b * 8, b * 8 + 8)
-        pack, own = hw_v[rows, :], first_v[rows, :]
+        pack, own = hw[rows, :], own_first[rows, :]
         both = jnp.minimum(pltpu.roll(pack, 112, 1), pltpu.roll(own, 112, 1))
         far, near = face(both, level, pltpu.roll(pack, 120, 1))
         west_h[rows, :] = pack * near - own * far
-        pack, own = he_v[rows, :], last_v[rows, :]
+        pack, own = he[rows, :], own_last[rows, :]
         both = jnp.minimum(pltpu.roll(pack, 112, 1), pltpu.roll(own, 112, 1))
         far, near = face(both, level, pltpu.roll(own, 120, 1))
         east_h[rows, :] = pack * far - own * near
     level = (row & 3).astype(F32)
     for j in range(LT):
         cols = slice(j * 128, j * 128 + 128)
-        far, near = face(jnp.minimum(s_v[16:24, cols], hn_v[16:24, cols]), level, s_v[8:16, cols])
-        north_h[:, cols] = hn_v[0:8, cols] * far - s_v[0:8, cols] * near
-        far, near = face(jnp.minimum(n_v[16:24, cols], hs_v[16:24, cols]), level, hs_v[8:16, cols])
-        south_h[:, cols] = hs_v[0:8, cols] * near - n_v[0:8, cols] * far
+        far, near = face(jnp.minimum(own_s[16:24, cols], hn_v[16:24, cols]), level, own_s[8:16, cols])
+        north_h[:, cols] = hn_v[0:8, cols] * far - own_s[0:8, cols] * near
+        far, near = face(jnp.minimum(own_n[16:24, cols], hs_v[16:24, cols]), level, hs_v[8:16, cols])
+        south_h[:, cols] = hs_v[0:8, cols] * near - own_n[0:8, cols] * far
 
     def rhs(j, n, b):
         rows = slice(b * 8, b * 8 + 8)
@@ -787,24 +773,14 @@
         return value
 
     for j in range(LT):
-        for c in fetch(j):
-            c.wait()
         if j == 2:
-            get_ice.wait()
+            put_ice.wait()
             for slot in range(SLOTS):
 
                 @pl.when(info[slot] >= 0)
                 def _(slot=slot):
                     patch(slot).start()
 
-        if j == 4:
-            for slot in range(SLOTS):
-
-                @pl.when(info[slot] >= 0)
-                def _(slot=slot):
-                    patch(slot).wait()
-
-            put_ice.start()
         for b in range(NB):
             rows = slice(b * 8, b * 8 + 8)
             own = d_v[j, rows, :]
@@ -831,12 +807,17 @@
 
     for j in range(LT):
         put(j).wait()
-    put_ice.wait()
+    for slot in range(SLOTS):
+
+        @pl.when(info[slot] >= 0)
+        def _(slot=slot):
+            patch(slot).wait()
 
 
 def ocean(n_lon, n_lat, *operands):
     anywhere = pl.BlockSpec(memory_space=pl.ANY)
     smem = pl.BlockSpec(memory_space=pltpu.SMEM)
+    inside = pl.BlockSpec(memory_space=pltpu.VMEM)
     column = pltpu.VMEM((ROWS, 128), F32)
     rows = pltpu.VMEM((24, COLS), F32)
 
@@ -850,33 +831,21 @@
             jax.ShapeDtypeStruct((2, LEV, ROWS, COLS), F32),
             jax.ShapeDtypeStruct((2, ROWS, COLS), F32),
         ),
-        in_specs=[smem, smem] + [anywhere] * (len(operands) - 2),
+        in_specs=[smem, smem] + [inside] * (len(operands) - 2),
         out_specs=(anywhere, anywhere),
         scratch_shapes=[
-            pltpu.VMEM((LT, 8, ROWS, 128), F32),
-            pltpu.VMEM((LT, ROWS, 128), I32),
-            pltpu.VMEM((LT, LEV, ROWS, 128), F32),
             pltpu.VMEM((LT, 2, LEV, ROWS, 128), F32),
-            pltpu.VMEM((2, ROWS, COLS), F32),
-            column,
-            column,
             rows,
             rows,
-            column,
-            column,
-            rows,
-            rows,
-            pltpu.VMEM((2, n_lon // 2, LT + 1, 8, 128), F32),
             pltpu.VMEM((LT + 1, 16, 128), F32),
             column,
             column,
             pltpu.VMEM((8, COLS), F32),
             pltpu.VMEM((8, COLS), F32),
-            pltpu.SemaphoreType.DMA((3, LT)),
             pltpu.SemaphoreType.DMA((LT,)),
-            pltpu.SemaphoreType.DMA((11 + SLOTS,)),
+            pltpu.SemaphoreType.DMA((1 + SLOTS,)),
         ],
-        compiler_params=pltpu.CompilerParams(vmem_limit_bytes=20 * 2**20),
+        compiler_params=pltpu.CompilerParams(vmem_limit_bytes=10 * 2**20),
     )(*operands)
 
 
@@ -884,10 +853,10 @@
     n_lon, n_lat = lax.axis_size("lon"), lax.axis_size("lat")
     in_hbm = [
         pltpu.with_memory_space_constraint(value, pltpu.HBM)
-        for value in (owned, state, depth, ivel, mass, strength, mask)
+        for value in (owned, state, depth, ivel, mass, strength, mask, vmix)
     ]
-    *rims, interim, res, info = exchange_and_ice(n_lon, n_lat, *in_hbm)
-    return ocean(n_lon, n_lat, partner, info, interim, depth, vmix, ivel, *rims, res)
+    *rims, interim, vmix_in, depth_in, ivel_in, res, info = exchange_and_ice(n_lon, n_lat, *in_hbm)
+    return ocean(n_lon, n_lat, partner, info, interim, vmix_in, depth_in, ivel_in, *rims, res)
 
 
 def solution(mesh):

time: 32.5 us -> 30.3 us (0.932)
  Pallas kernels: 31.7 us -> 29.5 us
    pallas_call x1, Pallas kernels: 6.21 us -> 3.88 us  [ocean(): pl.pallas_call(body, name='ocean', out_shape=(jax.ShapeDtypeStruct((2, LE...]
where the time goes in v3:
time: 30.3 us; the launch traced here: 30.2 us
  Pallas kernels  29.5 us (97%)
  between operations  0.66 us (2%)
    pallas_call x1, Pallas kernels, exchange_and_ice(): pl.pallas_call(body, name='exchange_and_ice', out_shape=(column, column,...  25.6 us
    pallas_call x1, Pallas kernels, ocean(): pl.pallas_call(body, name='ocean', out_shape=(jax.ShapeDtypeStruct((2, LE...  3.88 us

profile of v3, /device:TPU:70, one launch (start us, length us, event | category | flops | bytes accessed | tf_op | source)
XLA Modules:
  0.0 30.2 jit_solution(18375176284278828677)
XLA Ops:
  0.6 0.0 copy-start
  0.6 25.6 %exchange_and_ice.1 = (f32[128,128]{1,0:T(8,128)S(1)}, f32[128,128]{1,0:T(8,128)S(1)}, f32[24,1024]{1,0:T(8,128)S(1)}, f32[24,1024]{1,0:T(8,128)S(1)}, f32[128,1...) custom-call(s32[1,1,3]{2,1,0:T(1,128)} %refs_0_.2, ...), custom_call_target="tpu_custom_call" | custom-call | tf_op jit(solution)/shard_map/exchange_and_ice/pallas_call | solution.py:583
  26.3 0.0 copy-done
  26.3 3.9 %ocean.1 = (f32[2,4,128,1024]{3,2,1,0:T(8,128)}, f32[2,128,1024]{2,1,0:T(8,128)}) custom-call(s32[1024]{0:T(1024)S(1)} %copy-done, s32[3]{0:T(128)S(1)} %get-tuple-element.17.refs_1_, f32[8,8,128,128]{3,2,1,0:T(8,128)S(1)} %get-tuple-element.18.refs_2_, f32[8,4,128,128]{3,2,1,0:T(8,128)S(1)} %get-tuple-element.19.refs_3_, ...), custom_call_target="tpu_custom_call" | custom-call | tf_op jit(solution)/shard_map/ocean/pallas_call | solution.py:827
Async XLA Ops:
  0.6 25.6 %copy-start = (s32[1024]{0:T(1024)S(1)}, s32[1024]{0:T(1024)}, u32[]{:S(2)}) copy-start(s32[1024]{0:T(1024)} %refs_0_.3) | copy-start | bytes 12292

commit v4 on v3

--- a/solution.py
+++ b/solution.py
@@ -417,7 +417,7 @@
             for c in fetch(j + 1):
                 c.wait()
 
-        @pl.when(j == 2)
+        @pl.when(j == 4)
         def _():
             barrier_wait()
             list_1.start()
@@ -534,7 +534,7 @@
         places.append(jnp.clip(column_id - x * LT, 0, LT - 1))
 
     def hook(i):
-        @pl.when(jnp.logical_and(top, i == 2))
+        @pl.when(jnp.logical_and(top, i == 4))
         def _():
             own_fold.wait()
             for step in steps:

time: 30.3 us -> 31.8 us (1.050)
  Pallas kernels: 29.5 us -> 30.8 us
    pallas_call x1, Pallas kernels: 25.6 us -> 27 us  [exchange_and_ice(): pl.pallas_call(body, name='exchange_and_ice', out_shape=(column, column,...]
where the time goes in v4:
time: 31.8 us; the launch traced here: 31.5 us
  Pallas kernels  30.8 us (97%)
  between operations  0.66 us (2%)
    pallas_call x1, Pallas kernels, exchange_and_ice(): pl.pallas_call(body, name='exchange_and_ice', out_shape=(column, column,...  27 us
    pallas_call x1, Pallas kernels, ocean(): pl.pallas_call(body, name='ocean', out_shape=(jax.ShapeDtypeStruct((2, LE...  3.79 us

profile of v4, /device:TPU:70, one launch (start us, length us, event | category | flops | bytes accessed | tf_op | source)
XLA Modules:
  0.0 31.5 jit_solution(1607373612830054913)
XLA Ops:
  0.6 0.0 copy-start
  0.6 27.0 %exchange_and_ice.1 = (f32[128,128]{1,0:T(8,128)S(1)}, f32[128,128]{1,0:T(8,128)S(1)}, f32[24,1024]{1,0:T(8,128)S(1)}, f32[24,1024]{1,0:T(8,128)S(1)}, f32[128,1...) custom-call(s32[1,1,3]{2,1,0:T(1,128)} %refs_0_.2, ...), custom_call_target="tpu_custom_call" | custom-call | tf_op jit(solution)/shard_map/exchange_and_ice/pallas_call | solution.py:583
  27.7 0.0 copy-done
  27.7 3.8 %ocean.1 = (f32[2,4,128,1024]{3,2,1,0:T(8,128)}, f32[2,128,1024]{2,1,0:T(8,128)}) custom-call(s32[1024]{0:T(1024)S(1)} %copy-done, s32[3]{0:T(128)S(1)} %get-tuple-element.17.refs_1_, f32[8,8,128,128]{3,2,1,0:T(8,128)S(1)} %get-tuple-element.18.refs_2_, f32[8,4,128,128]{3,2,1,0:T(8,128)S(1)} %get-tuple-element.19.refs_3_, ...), custom_call_target="tpu_custom_call" | custom-call | tf_op jit(solution)/shard_map/ocean/pallas_call | solution.py:827
Async XLA Ops:
  0.6 27.0 %copy-start = (s32[1024]{0:T(1024)S(1)}, s32[1024]{0:T(1024)}, u32[]{:S(2)}) copy-start(s32[1024]{0:T(1024)} %refs_0_.3) | copy-start | bytes 12292

commit v5 on v4

--- a/solution.py
+++ b/solution.py
@@ -417,7 +417,7 @@
             for c in fetch(j + 1):
                 c.wait()
 
-        @pl.when(j == 4)
+        @pl.when(j == 2)
         def _():
             barrier_wait()
             list_1.start()

time: 31.8 us -> 30.3 us (0.953)
  Pallas kernels: 30.8 us -> 29.5 us
    pallas_call x1, Pallas kernels: 27 us -> 25.6 us  [exchange_and_ice(): pl.pallas_call(body, name='exchange_and_ice', out_shape=(column, column,...]
where the time goes in v5:
time: 30.3 us; the launch traced here: 30.2 us
  Pallas kernels  29.5 us (97%)
  between operations  0.66 us (2%)
    pallas_call x1, Pallas kernels, exchange_and_ice(): pl.pallas_call(body, name='exchange_and_ice', out_shape=(column, column,...  25.6 us
    pallas_call x1, Pallas kernels, ocean(): pl.pallas_call(body, name='ocean', out_shape=(jax.ShapeDtypeStruct((2, LE...  3.93 us

profile of v5, /device:TPU:70, one launch (start us, length us, event | category | flops | bytes accessed | tf_op | source)
XLA Modules:
  0.0 30.2 jit_solution(1989081525408214188)
XLA Ops:
  0.6 0.0 copy-start
  0.6 25.6 %exchange_and_ice.1 = (f32[128,128]{1,0:T(8,128)S(1)}, f32[128,128]{1,0:T(8,128)S(1)}, f32[24,1024]{1,0:T(8,128)S(1)}, f32[24,1024]{1,0:T(8,128)S(1)}, f32[128,1...) custom-call(s32[1,1,3]{2,1,0:T(1,128)} %refs_0_.2, ...), custom_call_target="tpu_custom_call" | custom-call | tf_op jit(solution)/shard_map/exchange_and_ice/pallas_call | solution.py:583
  26.3 0.0 copy-done
  26.3 3.9 %ocean.1 = (f32[2,4,128,1024]{3,2,1,0:T(8,128)}, f32[2,128,1024]{2,1,0:T(8,128)}) custom-call(s32[1024]{0:T(1024)S(1)} %copy-done, s32[3]{0:T(128)S(1)} %get-tuple-element.17.refs_1_, f32[8,8,128,128]{3,2,1,0:T(8,128)S(1)} %get-tuple-element.18.refs_2_, f32[8,4,128,128]{3,2,1,0:T(8,128)S(1)} %get-tuple-element.19.refs_3_, ...), custom_call_target="tpu_custom_call" | custom-call | tf_op jit(solution)/shard_map/ocean/pallas_call | solution.py:827
Async XLA Ops:
  0.6 25.6 %copy-start = (s32[1024]{0:T(1024)S(1)}, s32[1024]{0:T(1024)}, u32[]{:S(2)}) copy-start(s32[1024]{0:T(1024)} %refs_0_.3) | copy-start | bytes 12292

commit v6 on v5

--- a/solution.py
+++ b/solution.py
@@ -417,7 +417,7 @@
             for c in fetch(j + 1):
                 c.wait()
 
-        @pl.when(j == 2)
+        @pl.when(j == 1)
         def _():
             barrier_wait()
             list_1.start()

time: 30.3 us -> 29.9 us (0.987); the launches traced: 30.2 us -> 29.4 us
  Pallas kernels: 29.5 us -> 28.7 us
    pallas_call x1, Pallas kernels: 25.6 us -> 24.9 us  [exchange_and_ice(): pl.pallas_call(body, name='exchange_and_ice', out_shape=(column, column,...]
where the time goes in v6:
time: 29.9 us; the launch traced here: 29.4 us
  Pallas kernels  28.7 us (96%)
  between operations  0.66 us (2%)
    pallas_call x1, Pallas kernels, exchange_and_ice(): pl.pallas_call(body, name='exchange_and_ice', out_shape=(column, column,...  24.9 us
    pallas_call x1, Pallas kernels, ocean(): pl.pallas_call(body, name='ocean', out_shape=(jax.ShapeDtypeStruct((2, LE...  3.79 us

profile of v6, /device:TPU:70, one launch (start us, length us, event | category | flops | bytes accessed | tf_op | source)
XLA Modules:
  0.0 29.4 jit_solution(4970435045690984249)
XLA Ops:
  0.6 0.0 copy-start
  0.6 24.9 %exchange_and_ice.1 = (f32[128,128]{1,0:T(8,128)S(1)}, f32[128,128]{1,0:T(8,128)S(1)}, f32[24,1024]{1,0:T(8,128)S(1)}, f32[24,1024]{1,0:T(8,128)S(1)}, f32[128,1...) custom-call(s32[1,1,3]{2,1,0:T(1,128)} %refs_0_.2, ...), custom_call_target="tpu_custom_call" | custom-call | tf_op jit(solution)/shard_map/exchange_and_ice/pallas_call | solution.py:583
  25.6 0.0 copy-done
  25.6 3.8 %ocean.1 = (f32[2,4,128,1024]{3,2,1,0:T(8,128)}, f32[2,128,1024]{2,1,0:T(8,128)}) custom-call(s32[1024]{0:T(1024)S(1)} %copy-done, s32[3]{0:T(128)S(1)} %get-tuple-element.17.refs_1_, f32[8,8,128,128]{3,2,1,0:T(8,128)S(1)} %get-tuple-element.18.refs_2_, f32[8,4,128,128]{3,2,1,0:T(8,128)S(1)} %get-tuple-element.19.refs_3_, ...), custom_call_target="tpu_custom_call" | custom-call | tf_op jit(solution)/shard_map/ocean/pallas_call | solution.py:827
Async XLA Ops:
  0.6 24.9 %copy-start = (s32[1024]{0:T(1024)S(1)}, s32[1024]{0:T(1024)}, u32[]{:S(2)}) copy-start(s32[1024]{0:T(1024)} %refs_0_.3) | copy-start | bytes 12292
